TPU v7x, 256 devices: a whole 4x4x8 slice. The times are simulated.
256 devices in a mesh: gx: 16 (over z, core), gy: 16 (over x, y).
Axes of the slice: x: 4, y: 4, z: 8, core: 2. Of those that a mesh axis runs over, the one named last changes fastest.
Arguments:
- deflation: float32 [16, 16, 32, 16384], P('gx', 'gy'), may hold values from -0.1953125 to 0.1953125
- diag_stiff: float32 [16, 16, 16384], P('gx', 'gy'), may hold values from 3 to 12
- tile_vals: bfloat16 [16, 16, 128, 2, 128, 128], P('gx', 'gy'), may hold values from -1.25 to 1.25
- tile_cols: int32 [16, 16, 128, 2], P('gx', 'gy'), may hold values from 0 to 127
- west_coup: bfloat16 [16, 16, 32, 128, 128], P('gx', 'gy'), may hold values from -1.6970563 to 2.6970563
- north_coup: bfloat16 [16, 16, 32, 128, 128], P('gx', 'gy'), may hold values from -1.6970563 to 2.6970563
Outputs:
- coarse_blocks: float32 [16, 16, 3, 32, 32], P('gx', 'gy')
- pivots: float32 [16, 16, 32, 32], P('gx', 'gy')
- multipliers: float32 [16, 16, 32, 32], P('gx', 'gy')
All inputs are finite; a program needn't handle non-finite values.
Results may differ from a plain program's by a relative error of at most 0.0003.
The roundings to bfloat16 on the way count: a program that leaves them out, or rounds other values in their place, can miss the bound.
Values sent between devices are 32-bit elements; how exact they have to be, the bound alone decides.
A program may use at most 64 MiB of HBM per device.

v0:
```python
import jax
import jax.numpy as jnp
from jax import lax
from jax.sharding import PartitionSpec as P

HIGHEST = lax.Precision.HIGHEST


def passed_along(value, axis, steps):
    count = lax.axis_size(axis)
    first, last = (max(0, -steps), min(count, count - steps))
    return lax.ppermute(value, axis, [(source, source + steps) for source in range(first, last)])


def schur_step(previous, diag_block, low_block):
    factor = jnp.linalg.cholesky(previous)
    solved = jax.scipy.linalg.cho_solve((factor, True), low_block.T)
    multiplier = solved.T
    pivot_block = diag_block - jnp.dot(multiplier, low_block.T, precision=HIGHEST)
    return (pivot_block, multiplier)


def local(deflation, diag_stiff, tile_vals, tile_cols, west_coup, north_coup):
    vectors = deflation[0, 0]
    count_vec, row_total = vectors.shape
    tile_size = tile_vals.shape[-1]
    tile_count = row_total // tile_size
    band_tiles = west_coup.shape[2]
    band_rows = band_tiles * tile_size
    vector_tiles = vectors.reshape(count_vec, tile_count, tile_size)
    rounded = vector_tiles.astype(jnp.bfloat16)
    west_proj = jnp.einsum(
        "kfs,fst->fkt",
        rounded[:, 0:band_tiles],
        west_coup[0, 0],
        preferred_element_type=jnp.float32,
    )
    north_proj = jnp.einsum(
        "kfs,fst->fkt",
        rounded[:, 2 * band_tiles : 3 * band_tiles],
        north_coup[0, 0],
        preferred_element_type=jnp.float32,
    )
    east_band = vectors[:, band_rows : 2 * band_rows]
    south_band = vectors[:, 3 * band_rows : 4 * band_rows]
    from_west = passed_along(east_band, "gy", 1).reshape(count_vec, band_tiles, tile_size)
    from_north = passed_along(south_band, "gx", 1).reshape(count_vec, band_tiles, tile_size)
    west_block = -jnp.einsum("fkt,lft->kl", west_proj, from_west, precision=HIGHEST)
    north_block = -jnp.einsum("fkt,lft->kl", north_proj, from_north, precision=HIGHEST)
    applied = jnp.einsum(
        "krs,rjst->rjkt", rounded, tile_vals[0, 0], preferred_element_type=jnp.float32
    )
    partners = vector_tiles[:, tile_cols[0, 0]]
    cross_term = jnp.einsum("rjkt,lrjt->kl", applied, partners, precision=HIGHEST)
    gram_part = jnp.dot(vectors * diag_stiff[0, 0][None, :], vectors.T, precision=HIGHEST)
    self_blk = gram_part + cross_term + cross_term.T
    position = lax.axis_index("gy")
    line_len = lax.axis_size("gy")

    def relay(turn_index, state_pair):
        pivot_block, multiplier = state_pair
        previous = passed_along(pivot_block, "gy", 1)
        fresh_pivot, fresh_mult = schur_step(previous, self_blk, west_block)
        chosen = position == turn_index + 1
        return (
            jnp.where(chosen, fresh_pivot, pivot_block),
            jnp.where(chosen, fresh_mult, multiplier),
        )

    pivot_block, multiplier = lax.fori_loop(
        0, line_len - 1, relay, (self_blk, jnp.zeros_like(self_blk))
    )
    coarse = jnp.stack([self_blk, west_block, north_block], axis=0)
    return (coarse[None, None], pivot_block[None, None], multiplier[None, None])


def solution(mesh):
    placed = (
        P("gx", "gy", None, None),
        P("gx", "gy", None),
        P("gx", "gy", None, None, None, None),
        P("gx", "gy", None, None),
        P("gx", "gy", None, None, None),
        P("gx", "gy", None, None, None),
    )
    return jax.shard_map(
        local,
        mesh=mesh,
        in_specs=placed,
        out_specs=(
            P("gx", "gy", None, None, None),
            P("gx", "gy", None, None),
            P("gx", "gy", None, None),
        ),
        check_vma=False,
    )
```

profile of v0, /device:TPU:6, one launch (start us, length us, event | category | flops | bytes accessed | tf_op | source)
XLA Modules:
  0.0 269.2 jit_solution(2501891297272547452)
XLA Ops:
  3.0 3.5 %collective-permute-start.1 = (f32[32,4096]{1,0:T(8,128)}, f32[32,4096]{1,0:T(8,128)}, u32[]{:S(2)}, u32[]{:S(2)}) collective-permute-start(f32[32,4096]{1,0:T(8,128)} %get-tuple-element.168), channel_id=1, source_target_pairs={{0,1},{1,2},{2,3},{3,4},{4,5},{5,6},{6,7},{7,8},{8,9},{9,10},{10,1... | collective-permute-start | bytes 1572872 | tf_op jit(solution)/shard_map/ppermute | solution.py:12
  13.6 7.8 %fusion.7 = f32[128,2,128,32]{2,3,0,1:T(8,128)} fusion(f32[32,128,128]{2,1,0:T(8,128)} %bitcast.121, bf16[1,1,128,2,128,128]{5,4,3,2,1,0:T(8,128)(2,1)} %param.10), kind=kOutput, calls=%fused_computation.16 | convolution fusion | flops 268435456 | bytes 14680064 | tf_op jit(solution)/shard_map/krs,rjst->rjkt/dot_general | solution.py:50
  21.4 3.0 %gather_fusion = f32[256,32,128]{2,1,0:T(8,128)} fusion(f32[32,128,128]{2,0,1:T(8,128)S(1)} %copy.29, s32[1024]{0:T(1024)S(1)} %pad_clamp_fusion), kind=kCustom, calls=%fused_computation | custom fusion | bytes 8389632 | tf_op jit(solution)/shard_map/gather | solution.py:53
  24.3 7.1 %fusion.15 = f32[32,32]{1,0:T(8,128)S(1)} fusion(f32[32,128,2,128]{3,0,2,1:T(8,128)} %bitcast.119, f32[128,2,128,32]{2,3,0,1:T(8,128)} %fusion.7), kind=kOutput, calls=%fused_computation.24 | convolution fusion | flops 402653184 | bytes 8392704 | tf_op jit(solution)/shard_map/rjkt,lrjt->kl/dot_general | solution.py:54
  35.3 2.5 fusion.29
  39.4 226.0 %while.16 = (s32[]{:T(128)}, f32[32,32]{0,1:T(8,128)S(1)}, f32[32,32]{0,1:T(8,128)S(1)}, s32[]{:T(128)}, f32[32,32]{1,0:T(8,128)S(1)}, /*index=5*/f32[32,32]{0,1:T(8,128)S(1)}, s32[]{:T(128)}, s32[]{:T(128)}) while((s32[]{:T(128)}, f32[32,32]{0,1:T(8,128)S(1)}, f32[32,32]{0,1:T(8,128)S(1)}, s32[]{:T(128)}, f32[32,32]{1,0:T(8,128)S(1)}, ...), condition=%wide.region_3.4_spmd.clone, body=%wide.region_0.3_spmd.clone.sunk | while | flops 1192995 | bytes 102812 | solution.py:70
  39.4 3.5 %collective-permute-start = (f32[32,32]{0,1:T(8,128)S(1)}, f32[32,32]{0,1:T(8,128)S(1)}, u32[]{:S(2)}, u32[]{:S(2)}) collective-permute-start(f32[32,32]{0,1:T(8,128)S(1)} %get-tuple-element.220), channel_id=1, source_target_pairs={{0,1},{1,2},{2,3},{3,4},{4,5},{5,6},{6,7},{7,8},{8,9},{9,10},{10,1... | collective-permute-start | bytes 12296 | tf_op jit(solution)/shard_map/while/body/eval_jaxpr/ppermute | solution.py:12
  42.9 4.2 %collective-permute-done = f32[32,32]{0,1:T(8,128)S(1)} collective-permute-done((f32[32,32]{0,1:T(8,128)S(1)}, f32[32,32]{0,1:T(8,128)S(1)}, u32[]{:S(2)}, u32[]{:S(2)}) %collective-permute-start) | collective-permute-done | bytes 4128 | tf_op jit(solution)/shard_map/while/body/eval_jaxpr/ppermute | solution.py:12
  47.3 2.9 %cholesky.68 = f32[32,32]{1,0:T(8,128)S(1)} custom-call(f32[32,32]{1,0:T(8,128)S(1)} %fusion.70), custom_call_target="Cholesky" | custom-call | tf_op jit(solution)/shard_map/while/body/eval_jaxpr/jit(cholesky)/cholesky | solution.py:16
  51.5 2.4 custom-call.23
  56.4 5.8 %collective-permute-done = f32[32,32]{0,1:T(8,128)S(1)} collective-permute-done((f32[32,32]{0,1:T(8,128)S(1)}, f32[32,32]{0,1:T(8,128)S(1)}, u32[]{:S(2)}, u32[]{:S(2)}) %collective-permute-start) | collective-permute-done | bytes 4128 | tf_op jit(solution)/shard_map/while/body/eval_jaxpr/ppermute | solution.py:12
  62.3 2.9 %cholesky.68 = f32[32,32]{1,0:T(8,128)S(1)} custom-call(f32[32,32]{1,0:T(8,128)S(1)} %fusion.70), custom_call_target="Cholesky" | custom-call | tf_op jit(solution)/shard_map/while/body/eval_jaxpr/jit(cholesky)/cholesky | solution.py:16
  66.6 2.4 custom-call.23
  71.5 5.8 %collective-permute-done = f32[32,32]{0,1:T(8,128)S(1)} collective-permute-done((f32[32,32]{0,1:T(8,128)S(1)}, f32[32,32]{0,1:T(8,128)S(1)}, u32[]{:S(2)}, u32[]{:S(2)}) %collective-permute-start) | collective-permute-done | bytes 4128 | tf_op jit(solution)/shard_map/while/body/eval_jaxpr/ppermute | solution.py:12
  77.4 2.9 %cholesky.68 = f32[32,32]{1,0:T(8,128)S(1)} custom-call(f32[32,32]{1,0:T(8,128)S(1)} %fusion.70), custom_call_target="Cholesky" | custom-call | tf_op jit(solution)/shard_map/while/body/eval_jaxpr/jit(cholesky)/cholesky | solution.py:16
  81.6 2.4 custom-call.23
  86.6 5.8 %collective-permute-done = f32[32,32]{0,1:T(8,128)S(1)} collective-permute-done((f32[32,32]{0,1:T(8,128)S(1)}, f32[32,32]{0,1:T(8,128)S(1)}, u32[]{:S(2)}, u32[]{:S(2)}) %collective-permute-start) | collective-permute-done | bytes 4128 | tf_op jit(solution)/shard_map/while/body/eval_jaxpr/ppermute | solution.py:12
  92.5 2.9 %cholesky.68 = f32[32,32]{1,0:T(8,128)S(1)} custom-call(f32[32,32]{1,0:T(8,128)S(1)} %fusion.70), custom_call_target="Cholesky" | custom-call | tf_op jit(solution)/shard_map/while/body/eval_jaxpr/jit(cholesky)/cholesky | solution.py:16
  96.7 2.4 custom-call.23
  101.6 5.8 %collective-permute-done = f32[32,32]{0,1:T(8,128)S(1)} collective-permute-done((f32[32,32]{0,1:T(8,128)S(1)}, f32[32,32]{0,1:T(8,128)S(1)}, u32[]{:S(2)}, u32[]{:S(2)}) %collective-permute-start) | collective-permute-done | bytes 4128 | tf_op jit(solution)/shard_map/while/body/eval_jaxpr/ppermute | solution.py:12
  107.5 2.9 %cholesky.68 = f32[32,32]{1,0:T(8,128)S(1)} custom-call(f32[32,32]{1,0:T(8,128)S(1)} %fusion.70), custom_call_target="Cholesky" | custom-call | tf_op jit(solution)/shard_map/while/body/eval_jaxpr/jit(cholesky)/cholesky | solution.py:16
  111.8 2.4 custom-call.23
  116.7 5.8 %collective-permute-done = f32[32,32]{0,1:T(8,128)S(1)} collective-permute-done((f32[32,32]{0,1:T(8,128)S(1)}, f32[32,32]{0,1:T(8,128)S(1)}, u32[]{:S(2)}, u32[]{:S(2)}) %collective-permute-start) | collective-permute-done | bytes 4128 | tf_op jit(solution)/shard_map/while/body/eval_jaxpr/ppermute | solution.py:12
  122.6 2.9 %cholesky.68 = f32[32,32]{1,0:T(8,128)S(1)} custom-call(f32[32,32]{1,0:T(8,128)S(1)} %fusion.70), custom_call_target="Cholesky" | custom-call | tf_op jit(solution)/shard_map/while/body/eval_jaxpr/jit(cholesky)/cholesky | solution.py:16
  126.8 2.4 custom-call.23
  131.8 5.8 %collective-permute-done = f32[32,32]{0,1:T(8,128)S(1)} collective-permute-done((f32[32,32]{0,1:T(8,128)S(1)}, f32[32,32]{0,1:T(8,128)S(1)}, u32[]{:S(2)}, u32[]{:S(2)}) %collective-permute-start) | collective-permute-done | bytes 4128 | tf_op jit(solution)/shard_map/while/body/eval_jaxpr/ppermute | solution.py:12
  137.6 2.9 %cholesky.68 = f32[32,32]{1,0:T(8,128)S(1)} custom-call(f32[32,32]{1,0:T(8,128)S(1)} %fusion.70), custom_call_target="Cholesky" | custom-call | tf_op jit(solution)/shard_map/while/body/eval_jaxpr/jit(cholesky)/cholesky | solution.py:16
  141.9 2.4 custom-call.23
  146.8 5.8 %collective-permute-done = f32[32,32]{0,1:T(8,128)S(1)} collective-permute-done((f32[32,32]{0,1:T(8,128)S(1)}, f32[32,32]{0,1:T(8,128)S(1)}, u32[]{:S(2)}, u32[]{:S(2)}) %collective-permute-start) | collective-permute-done | bytes 4128 | tf_op jit(solution)/shard_map/while/body/eval_jaxpr/ppermute | solution.py:12
  152.7 2.9 %cholesky.68 = f32[32,32]{1,0:T(8,128)S(1)} custom-call(f32[32,32]{1,0:T(8,128)S(1)} %fusion.70), custom_call_target="Cholesky" | custom-call | tf_op jit(solution)/shard_map/while/body/eval_jaxpr/jit(cholesky)/cholesky | solution.py:16
  157.0 2.4 custom-call.23
  161.9 5.8 %collective-permute-done = f32[32,32]{0,1:T(8,128)S(1)} collective-permute-done((f32[32,32]{0,1:T(8,128)S(1)}, f32[32,32]{0,1:T(8,128)S(1)}, u32[]{:S(2)}, u32[]{:S(2)}) %collective-permute-start) | collective-permute-done | bytes 4128 | tf_op jit(solution)/shard_map/while/body/eval_jaxpr/ppermute | solution.py:12
  167.8 2.9 %cholesky.68 = f32[32,32]{1,0:T(8,128)S(1)} custom-call(f32[32,32]{1,0:T(8,128)S(1)} %fusion.70), custom_call_target="Cholesky" | custom-call | tf_op jit(solution)/shard_map/while/body/eval_jaxpr/jit(cholesky)/cholesky | solution.py:16
  172.0 2.4 custom-call.23
  177.0 5.8 %collective-permute-done = f32[32,32]{0,1:T(8,128)S(1)} collective-permute-done((f32[32,32]{0,1:T(8,128)S(1)}, f32[32,32]{0,1:T(8,128)S(1)}, u32[]{:S(2)}, u32[]{:S(2)}) %collective-permute-start) | collective-permute-done | bytes 4128 | tf_op jit(solution)/shard_map/while/body/eval_jaxpr/ppermute | solution.py:12
  182.8 2.9 %cholesky.68 = f32[32,32]{1,0:T(8,128)S(1)} custom-call(f32[32,32]{1,0:T(8,128)S(1)} %fusion.70), custom_call_target="Cholesky" | custom-call | tf_op jit(solution)/shard_map/while/body/eval_jaxpr/jit(cholesky)/cholesky | solution.py:16
  187.1 2.4 custom-call.23
  192.0 5.8 %collective-permute-done = f32[32,32]{0,1:T(8,128)S(1)} collective-permute-done((f32[32,32]{0,1:T(8,128)S(1)}, f32[32,32]{0,1:T(8,128)S(1)}, u32[]{:S(2)}, u32[]{:S(2)}) %collective-permute-start) | collective-permute-done | bytes 4128 | tf_op jit(solution)/shard_map/while/body/eval_jaxpr/ppermute | solution.py:12
  197.9 2.9 %cholesky.68 = f32[32,32]{1,0:T(8,128)S(1)} custom-call(f32[32,32]{1,0:T(8,128)S(1)} %fusion.70), custom_call_target="Cholesky" | custom-call | tf_op jit(solution)/shard_map/while/body/eval_jaxpr/jit(cholesky)/cholesky | solution.py:16
  207.1 5.8 %collective-permute-done = f32[32,32]{0,1:T(8,128)S(1)} collective-permute-done((f32[32,32]{0,1:T(8,128)S(1)}, f32[32,32]{0,1:T(8,128)S(1)}, u32[]{:S(2)}, u32[]{:S(2)}) %collective-permute-start) | collective-permute-done | bytes 4128 | tf_op jit(solution)/shard_map/while/body/eval_jaxpr/ppermute | solution.py:12
  213.0 2.9 %cholesky.68 = f32[32,32]{1,0:T(8,128)S(1)} custom-call(f32[32,32]{1,0:T(8,128)S(1)} %fusion.70), custom_call_target="Cholesky" | custom-call | tf_op jit(solution)/shard_map/while/body/eval_jaxpr/jit(cholesky)/cholesky | solution.py:16
  222.2 5.8 %collective-permute-done = f32[32,32]{0,1:T(8,128)S(1)} collective-permute-done((f32[32,32]{0,1:T(8,128)S(1)}, f32[32,32]{0,1:T(8,128)S(1)}, u32[]{:S(2)}, u32[]{:S(2)}) %collective-permute-start) | collective-permute-done | bytes 4128 | tf_op jit(solution)/shard_map/while/body/eval_jaxpr/ppermute | solution.py:12
  228.0 2.9 %cholesky.68 = f32[32,32]{1,0:T(8,128)S(1)} custom-call(f32[32,32]{1,0:T(8,128)S(1)} %fusion.70), custom_call_target="Cholesky" | custom-call | tf_op jit(solution)/shard_map/while/body/eval_jaxpr/jit(cholesky)/cholesky | solution.py:16
  237.2 5.8 %collective-permute-done = f32[32,32]{0,1:T(8,128)S(1)} collective-permute-done((f32[32,32]{0,1:T(8,128)S(1)}, f32[32,32]{0,1:T(8,128)S(1)}, u32[]{:S(2)}, u32[]{:S(2)}) %collective-permute-start) | collective-permute-done | bytes 4128 | tf_op jit(solution)/shard_map/while/body/eval_jaxpr/ppermute | solution.py:12
  243.1 2.9 %cholesky.68 = f32[32,32]{1,0:T(8,128)S(1)} custom-call(f32[32,32]{1,0:T(8,128)S(1)} %fusion.70), custom_call_target="Cholesky" | custom-call | tf_op jit(solution)/shard_map/while/body/eval_jaxpr/jit(cholesky)/cholesky | solution.py:16
  252.3 5.8 %collective-permute-done = f32[32,32]{0,1:T(8,128)S(1)} collective-permute-done((f32[32,32]{0,1:T(8,128)S(1)}, f32[32,32]{0,1:T(8,128)S(1)}, u32[]{:S(2)}, u32[]{:S(2)}) %collective-permute-start) | collective-permute-done | bytes 4128 | tf_op jit(solution)/shard_map/while/body/eval_jaxpr/ppermute | solution.py:12
  258.2 2.9 %cholesky.68 = f32[32,32]{1,0:T(8,128)S(1)} custom-call(f32[32,32]{1,0:T(8,128)S(1)} %fusion.70), custom_call_target="Cholesky" | custom-call | tf_op jit(solution)/shard_map/while/body/eval_jaxpr/jit(cholesky)/cholesky | solution.py:16
  262.4 2.4 custom-call.23
  (173 shorter events, 84.2 us)
Async XLA Ops:
  0.6 30.8 %copy-start = (bf16[1,1,32,128,128]{4,3,2,1,0:T(8,128)(2,1)S(1)}, bf16[1,1,32,128,128]{4,3,2,1,0:T(8,128)(2,1)}, u32[]{:S(2)}) copy-start(bf16[1,1,32,128,128]{4,3,2,1,0:T(8,128)(2,1)} %param.12) | copy-start | bytes 3145732
  3.0 34.8 %collective-permute-start.1 = (f32[32,4096]{1,0:T(8,128)}, f32[32,4096]{1,0:T(8,128)}, u32[]{:S(2)}, u32[]{:S(2)}) collective-permute-start(f32[32,4096]{1,0:T(8,128)} %get-tuple-element.168), channel_id=1, source_target_pairs={{0,1},{1,2},{2,3},{3,4},{4,5},{5,6},{6,7},{7,8},{8,9},{9,10},{10,1... | collective-permute-start | bytes 1572872 | tf_op jit(solution)/shard_map/ppermute | solution.py:12
  6.5 260.3 %collective-permute-start.2 = (f32[32,4096]{1,0:T(8,128)}, f32[32,4096]{1,0:T(8,128)}, u32[]{:S(2)}, u32[]{:S(2)}) collective-permute-start(f32[32,4096]{1,0:T(8,128)} %get-tuple-element.169), channel_id=1, source_target_pairs={{0,16},{16,32},{32,48},{48,64},{64,80},{80,96},{96,112},{112,128},... | collective-permute-start | bytes 1572872 | tf_op jit(solution)/shard_map/ppermute | solution.py:12
  8.7 4.6 %copy-start.6 = (s32[1,1,128,2]{2,3,1,0:T(2,128)S(1)}, s32[1,1,128,2]{2,3,1,0:T(2,128)}, u32[]{:S(2)}) copy-start(s32[1,1,128,2]{2,3,1,0:T(2,128)} %param.11) | copy-start | bytes 3076
  10.7 1.4 copy-start.2
  24.3 7.1 %copy-start.3 = (f32[4,8,128,128]{3,2,1,0:T(8,128)S(1)}, f32[4,8,128,128]{3,2,1,0:T(8,128)}, u32[]{:S(2)}) copy-start(f32[4,8,128,128]{3,2,1,0:T(8,128)} %copy-done.2) | copy-start | bytes 6291460
  31.5 1.8 copy-start.1
  31.5 1.8 copy-start.5
  35.3 2.5 copy-start.4
  39.4 7.7 %collective-permute-start = (f32[32,32]{0,1:T(8,128)S(1)}, f32[32,32]{0,1:T(8,128)S(1)}, u32[]{:S(2)}, u32[]{:S(2)}) collective-permute-start(f32[32,32]{0,1:T(8,128)S(1)} %get-tuple-element.220), channel_id=1, source_target_pairs={{0,1},{1,2},{2,3},{3,4},{4,5},{5,6},{6,7},{7,8},{8,9},{9,10},{10,1... | collective-permute-start | bytes 12296 | tf_op jit(solution)/shard_map/while/body/eval_jaxpr/ppermute | solution.py:12
  54.5 7.7 %collective-permute-start = (f32[32,32]{0,1:T(8,128)S(1)}, f32[32,32]{0,1:T(8,128)S(1)}, u32[]{:S(2)}, u32[]{:S(2)}) collective-permute-start(f32[32,32]{0,1:T(8,128)S(1)} %get-tuple-element.220), channel_id=1, source_target_pairs={{0,1},{1,2},{2,3},{3,4},{4,5},{5,6},{6,7},{7,8},{8,9},{9,10},{10,1... | collective-permute-start | bytes 12296 | tf_op jit(solution)/shard_map/while/body/eval_jaxpr/ppermute | solution.py:12
  69.6 7.7 %collective-permute-start = (f32[32,32]{0,1:T(8,128)S(1)}, f32[32,32]{0,1:T(8,128)S(1)}, u32[]{:S(2)}, u32[]{:S(2)}) collective-permute-start(f32[32,32]{0,1:T(8,128)S(1)} %get-tuple-element.220), channel_id=1, source_target_pairs={{0,1},{1,2},{2,3},{3,4},{4,5},{5,6},{6,7},{7,8},{8,9},{9,10},{10,1... | collective-permute-start | bytes 12296 | tf_op jit(solution)/shard_map/while/body/eval_jaxpr/ppermute | solution.py:12
  84.6 7.7 %collective-permute-start = (f32[32,32]{0,1:T(8,128)S(1)}, f32[32,32]{0,1:T(8,128)S(1)}, u32[]{:S(2)}, u32[]{:S(2)}) collective-permute-start(f32[32,32]{0,1:T(8,128)S(1)} %get-tuple-element.220), channel_id=1, source_target_pairs={{0,1},{1,2},{2,3},{3,4},{4,5},{5,6},{6,7},{7,8},{8,9},{9,10},{10,1... | collective-permute-start | bytes 12296 | tf_op jit(solution)/shard_map/while/body/eval_jaxpr/ppermute | solution.py:12
  99.7 7.7 %collective-permute-start = (f32[32,32]{0,1:T(8,128)S(1)}, f32[32,32]{0,1:T(8,128)S(1)}, u32[]{:S(2)}, u32[]{:S(2)}) collective-permute-start(f32[32,32]{0,1:T(8,128)S(1)} %get-tuple-element.220), channel_id=1, source_target_pairs={{0,1},{1,2},{2,3},{3,4},{4,5},{5,6},{6,7},{7,8},{8,9},{9,10},{10,1... | collective-permute-start | bytes 12296 | tf_op jit(solution)/shard_map/while/body/eval_jaxpr/ppermute | solution.py:12
  114.8 7.7 %collective-permute-start = (f32[32,32]{0,1:T(8,128)S(1)}, f32[32,32]{0,1:T(8,128)S(1)}, u32[]{:S(2)}, u32[]{:S(2)}) collective-permute-start(f32[32,32]{0,1:T(8,128)S(1)} %get-tuple-element.220), channel_id=1, source_target_pairs={{0,1},{1,2},{2,3},{3,4},{4,5},{5,6},{6,7},{7,8},{8,9},{9,10},{10,1... | collective-permute-start | bytes 12296 | tf_op jit(solution)/shard_map/while/body/eval_jaxpr/ppermute | solution.py:12
  129.8 7.7 %collective-permute-start = (f32[32,32]{0,1:T(8,128)S(1)}, f32[32,32]{0,1:T(8,128)S(1)}, u32[]{:S(2)}, u32[]{:S(2)}) collective-permute-start(f32[32,32]{0,1:T(8,128)S(1)} %get-tuple-element.220), channel_id=1, source_target_pairs={{0,1},{1,2},{2,3},{3,4},{4,5},{5,6},{6,7},{7,8},{8,9},{9,10},{10,1... | collective-permute-start | bytes 12296 | tf_op jit(solution)/shard_map/while/body/eval_jaxpr/ppermute | solution.py:12
  144.9 7.7 %collective-permute-start = (f32[32,32]{0,1:T(8,128)S(1)}, f32[32,32]{0,1:T(8,128)S(1)}, u32[]{:S(2)}, u32[]{:S(2)}) collective-permute-start(f32[32,32]{0,1:T(8,128)S(1)} %get-tuple-element.220), channel_id=1, source_target_pairs={{0,1},{1,2},{2,3},{3,4},{4,5},{5,6},{6,7},{7,8},{8,9},{9,10},{10,1... | collective-permute-start | bytes 12296 | tf_op jit(solution)/shard_map/while/body/eval_jaxpr/ppermute | solution.py:12
  160.0 7.7 %collective-permute-start = (f32[32,32]{0,1:T(8,128)S(1)}, f32[32,32]{0,1:T(8,128)S(1)}, u32[]{:S(2)}, u32[]{:S(2)}) collective-permute-start(f32[32,32]{0,1:T(8,128)S(1)} %get-tuple-element.220), channel_id=1, source_target_pairs={{0,1},{1,2},{2,3},{3,4},{4,5},{5,6},{6,7},{7,8},{8,9},{9,10},{10,1... | collective-permute-start | bytes 12296 | tf_op jit(solution)/shard_map/while/body/eval_jaxpr/ppermute | solution.py:12
  175.0 7.7 %collective-permute-start = (f32[32,32]{0,1:T(8,128)S(1)}, f32[32,32]{0,1:T(8,128)S(1)}, u32[]{:S(2)}, u32[]{:S(2)}) collective-permute-start(f32[32,32]{0,1:T(8,128)S(1)} %get-tuple-element.220), channel_id=1, source_target_pairs={{0,1},{1,2},{2,3},{3,4},{4,5},{5,6},{6,7},{7,8},{8,9},{9,10},{10,1... | collective-permute-start | bytes 12296 | tf_op jit(solution)/shard_map/while/body/eval_jaxpr/ppermute | solution.py:12
  190.1 7.7 %collective-permute-start = (f32[32,32]{0,1:T(8,128)S(1)}, f32[32,32]{0,1:T(8,128)S(1)}, u32[]{:S(2)}, u32[]{:S(2)}) collective-permute-start(f32[32,32]{0,1:T(8,128)S(1)} %get-tuple-element.220), channel_id=1, source_target_pairs={{0,1},{1,2},{2,3},{3,4},{4,5},{5,6},{6,7},{7,8},{8,9},{9,10},{10,1... | collective-permute-start | bytes 12296 | tf_op jit(solution)/shard_map/while/body/eval_jaxpr/ppermute | solution.py:12
  205.1 7.7 %collective-permute-start = (f32[32,32]{0,1:T(8,128)S(1)}, f32[32,32]{0,1:T(8,128)S(1)}, u32[]{:S(2)}, u32[]{:S(2)}) collective-permute-start(f32[32,32]{0,1:T(8,128)S(1)} %get-tuple-element.220), channel_id=1, source_target_pairs={{0,1},{1,2},{2,3},{3,4},{4,5},{5,6},{6,7},{7,8},{8,9},{9,10},{10,1... | collective-permute-start | bytes 12296 | tf_op jit(solution)/shard_map/while/body/eval_jaxpr/ppermute | solution.py:12
  220.2 7.7 %collective-permute-start = (f32[32,32]{0,1:T(8,128)S(1)}, f32[32,32]{0,1:T(8,128)S(1)}, u32[]{:S(2)}, u32[]{:S(2)}) collective-permute-start(f32[32,32]{0,1:T(8,128)S(1)} %get-tuple-element.220), channel_id=1, source_target_pairs={{0,1},{1,2},{2,3},{3,4},{4,5},{5,6},{6,7},{7,8},{8,9},{9,10},{10,1... | collective-permute-start | bytes 12296 | tf_op jit(solution)/shard_map/while/body/eval_jaxpr/ppermute | solution.py:12
  235.3 7.7 %collective-permute-start = (f32[32,32]{0,1:T(8,128)S(1)}, f32[32,32]{0,1:T(8,128)S(1)}, u32[]{:S(2)}, u32[]{:S(2)}) collective-permute-start(f32[32,32]{0,1:T(8,128)S(1)} %get-tuple-element.220), channel_id=1, source_target_pairs={{0,1},{1,2},{2,3},{3,4},{4,5},{5,6},{6,7},{7,8},{8,9},{9,10},{10,1... | collective-permute-start | bytes 12296 | tf_op jit(solution)/shard_map/while/body/eval_jaxpr/ppermute | solution.py:12
  250.3 7.7 %collective-permute-start = (f32[32,32]{0,1:T(8,128)S(1)}, f32[32,32]{0,1:T(8,128)S(1)}, u32[]{:S(2)}, u32[]{:S(2)}) collective-permute-start(f32[32,32]{0,1:T(8,128)S(1)} %get-tuple-element.220), channel_id=1, source_target_pairs={{0,1},{1,2},{2,3},{3,4},{4,5},{5,6},{6,7},{7,8},{8,9},{9,10},{10,1... | collective-permute-start | bytes 12296 | tf_op jit(solution)/shard_map/while/body/eval_jaxpr/ppermute | solution.py:12
where the time goes:
time: 270 us; the launch traced here: 269 us
  other arithmetic  101 us (37%)
  waiting for transfers between devices  85.5 us (32%)
  starting transfers between devices  36.1 us (13%)
  matrix products  31.7 us (12%)
  local copies, waits for them, and re-layouts  13.3 us (5%)
    ppermute x17, waiting for transfers between devices, passed_along(): lax.ppermute(value, axis, [(source, source + steps) for source in range(f...  85.5 us
    another operation x45, other arithmetic, schur_step(): factor = jnp.linalg.cholesky(previous)  53.9 us
    another operation x30, other arithmetic, schur_step(): solved = jax.scipy.linalg.cho_solve((factor, True), low_block.T)  46.3 us
    ppermute x17, starting transfers between devices, passed_along(): lax.ppermute(value, axis, [(source, source + steps) for source in range(f...  36.1 us
    dot_general x1, matrix products, local(): jnp.einsum('krs,rjst->rjkt', rounded, tile_vals[0, 0], preferred_element_...  7.77 us
    dot_general x1, matrix products, local(): jnp.einsum('rjkt,lrjt->kl', applied, partners, precision=HIGHEST)  7.06 us
    another operation x30, matrix products, schur_step(): solved = jax.scipy.linalg.cho_solve((factor, True), low_block.T)  5.56 us
  transfers between devices with their start and end apart: 17, of which 15 were waited for; matrix products, arithmetic and copies ran while one was open for 52% of the time, Pallas kernels for 0%

commit v1 on v0

v1 whole, which is shorter than its diff:
```python
import functools

import jax
import jax.numpy as jnp
from jax import lax
from jax.experimental import pallas as pl
from jax.experimental.pallas import tpu as pltpu
from jax.sharding import PartitionSpec as P

MESH = pl.DeviceIdType.MESH
F32 = jnp.float32
BF16 = jnp.bfloat16
HIGHEST = lax.Precision.HIGHEST

K = 32
TS = 128
NT = 128
FT = 32
NL = NT * TS
ROW = 16
COL = 16
HALF = 16
WIDE = HALF * TS
CHUNKS = 16
PER = NT // CHUNKS
NT_DIMS = (((1,), (1,)), ((), ()))


def halves(values):
    high = values.astype(BF16)
    low = (values - high.astype(F32)).astype(BF16)
    return high, low


def stacked(values):
    high, low = halves(values)
    return jnp.concatenate([high, low], axis=0)


def folded(total):
    return (
        total[0:K, 0:K] + total[0:K, K : 2 * K] + total[K : 2 * K, 0:K] + total[K : 2 * K, K : 2 * K]
    )


def nt_dot(left, right):
    return lax.dot_general(left, right, NT_DIMS, preferred_element_type=F32)


def blocks_kernel(
    defl_hbm, diag_ref, vals_hbm, cols_ref, west_hbm, north_hbm,
    out_ref,
    vec, pair, vals, west, north, proj_w, proj_n,
    got_e, got_s, got_pw, got_pn, mine, slots, got_n, sent_n,
    sem_in, sem_vals, send_band, recv_band, send_row, recv_row, send_n, recv_n,
):
    row = lax.axis_index("gx")
    col = lax.axis_index("gy")
    east = {"gy": lax.rem(col + 1, COL)}
    west_of = {"gy": lax.rem(col + COL - 1, COL)}
    south = {"gx": lax.rem(row + 1, ROW)}
    north_of = {"gx": lax.rem(row + ROW - 1, ROW)}

    load_vec = pltpu.make_async_copy(defl_hbm.at[0, 0], vec, sem_in.at[0])
    load_west = pltpu.make_async_copy(west_hbm.at[0, 0], west, sem_in.at[1])
    load_north = pltpu.make_async_copy(north_hbm.at[0, 0], north, sem_in.at[2])
    load_vec.start()
    load_west.start()
    load_north.start()
    load_vals = []
    for c in range(CHUNKS):
        part = pl.ds(c * PER, PER)
        load_vals.append(
            pltpu.make_async_copy(vals_hbm.at[0, 0, part], vals.at[part], sem_vals.at[c])
        )
        load_vals[-1].start()

    barrier = pltpu.get_barrier_semaphore()
    for step in range(1, COL):
        pl.semaphore_signal(
            barrier, inc=1, device_id={"gy": lax.rem(col + step, COL)}, device_id_type=MESH
        )
    pl.semaphore_signal(barrier, inc=1, device_id=south, device_id_type=MESH)
    pl.semaphore_signal(barrier, inc=1, device_id=north_of, device_id_type=MESH)
    pl.semaphore_wait(barrier, COL + 1)

    def remote(source, target, at, device):
        copy = pltpu.make_async_remote_copy(
            src_ref=source,
            dst_ref=target,
            send_sem=send_band.at[at],
            recv_sem=recv_band.at[at],
            device_id=device,
            device_id_type=MESH,
        )
        copy.start()
        return copy

    move_e = remote(defl_hbm.at[0, 0, :, pl.ds(FT * TS, WIDE)], got_e, 0, east)
    move_s = remote(defl_hbm.at[0, 0, :, pl.ds(3 * FT * TS, WIDE)], got_s, 1, south)

    load_vec.wait()

    def split(c, total):
        part = pl.ds(pl.multiple_of(c * 1024, 1024), 1024)
        values = vec[:, part]
        both = stacked(values)
        for t in range(8):
            pair[c * 8 + t] = both[:, t * TS : (t + 1) * TS]
        scaled = stacked(values * (diag_ref[0, :, part] * 0.5))
        return total + nt_dot(scaled, both)

    total = lax.fori_loop(0, NL // 1024, split, jnp.zeros((2 * K, 2 * K), F32))

    def project(tiles, first, target):
        def one(f, carry):
            place = pl.ds(pl.multiple_of(f * TS, TS), TS)
            target[:, place] = jnp.dot(
                pair[first + f, 0:K], tiles[f], preferred_element_type=F32
            )
            return carry

        return one

    load_west.wait()
    lax.fori_loop(HALF, FT, project(west, 0, proj_w), 0, unroll=4)
    move_pw = remote(proj_w.at[:, pl.ds(WIDE, FT * TS - WIDE)], got_pw, 2, west_of)
    load_north.wait()
    lax.fori_loop(HALF, FT, project(north, 2 * FT, proj_n), 0, unroll=4)
    move_pn = remote(proj_n.at[:, pl.ds(WIDE, FT * TS - WIDE)], got_pn, 3, north_of)
    lax.fori_loop(0, HALF, project(west, 0, proj_w), 0, unroll=4)
    lax.fori_loop(0, HALF, project(north, 2 * FT, proj_n), 0, unroll=4)

    def tile_row(r, total):
        own = pair[r, 0:K]
        left, right = [], []
        for j in range(2):
            left.append(stacked(jnp.dot(own, vals[r, j], preferred_element_type=F32)))
            right.append(pair[cols_ref[0, 0, r, j]])
        return total + nt_dot(jnp.concatenate(left, axis=1), jnp.concatenate(right, axis=1))

    for c in range(CHUNKS):
        load_vals[c].wait()
        total = lax.fori_loop(c * PER, (c + 1) * PER, tile_row, total, unroll=8)
    cross = folded(total)
    self_block = cross + cross.T

    def band(left, left_at, right, right_at, count):
        def one(c, acc):
            a = left[:, pl.ds(pl.multiple_of(left_at + c * 512, 512), 512)]
            b = right[:, pl.ds(pl.multiple_of(right_at + c * 512, 512), 512)]
            return acc + nt_dot(stacked(a), stacked(b))

        return -folded(lax.fori_loop(0, count // 512, one, jnp.zeros((2 * K, 2 * K), F32)))

    move_e.wait_recv()
    west_here = jnp.where(col > 0, band(proj_w, 0, got_e, 0, WIDE), 0.0)
    move_pw.wait_recv()
    west_next = band(got_pw, 0, vec, FT * TS + WIDE, FT * TS - WIDE)
    move_pn.wait_recv()
    sent_n[:, 0:K] = band(got_pn, 0, vec, 3 * FT * TS + WIDE, FT * TS - WIDE)
    move_n = pltpu.make_async_remote_copy(
        src_ref=sent_n, dst_ref=got_n, send_sem=send_n, recv_sem=recv_n,
        device_id=south, device_id_type=MESH,
    )
    move_n.start()
    mine[...] = jnp.concatenate([self_block, west_here, west_next, west_next], axis=1)

    def to_row(step):
        return pltpu.make_async_remote_copy(
            src_ref=mine,
            dst_ref=slots.at[step - 1],
            send_sem=send_row.at[step - 1],
            recv_sem=recv_row.at[step - 1],
            device_id={"gy": lax.rem(col + step, COL)},
            device_id_type=MESH,
        )

    for step in range(1, COL):
        @pl.when(col + step < COL)
        def _():
            to_row(step).start()

    move_s.wait_recv()
    north_here = band(proj_n, 0, got_s, 0, WIDE)
    move_n.wait_recv()
    north_block = jnp.where(row > 0, north_here + got_n[:, 0:K], 0.0)
    out_ref[COL - 1] = jnp.concatenate(
        [self_block, west_here, west_next, north_block], axis=1
    )

    for step in range(1, COL):
        @pl.when(col >= step)
        def _():
            to_row(step).wait_recv()
            out_ref[step - 1] = slots[step - 1]

        @pl.when(col < step)
        def _():
            out_ref[step - 1] = jnp.zeros((K, 4 * K), F32)

        @pl.when(col + step < COL)
        def _():
            to_row(step).wait_send()

    move_e.wait_send()
    move_s.wait_send()
    move_pw.wait_send()
    move_pn.wait_send()
    move_n.wait_send()


def made_blocks(defl, diag, vals, cols, west, north):
    hbm = pl.BlockSpec(memory_space=pl.ANY)
    vmem = pl.BlockSpec(memory_space=pltpu.VMEM)
    return pl.pallas_call(
        blocks_kernel,
        out_shape=jax.ShapeDtypeStruct((COL, K, 4 * K), F32),
        in_specs=[hbm, vmem, hbm, pl.BlockSpec(memory_space=pltpu.SMEM), hbm, hbm],
        out_specs=vmem,
        scratch_shapes=[
            pltpu.VMEM((K, NL), F32),
            pltpu.VMEM((NT, 2 * K, TS), BF16),
            pltpu.VMEM((NT, 2, TS, TS), BF16),
            pltpu.VMEM((FT, TS, TS), BF16),
            pltpu.VMEM((FT, TS, TS), BF16),
            pltpu.VMEM((K, FT * TS), F32),
            pltpu.VMEM((K, FT * TS), F32),
            pltpu.VMEM((K, WIDE), F32),
            pltpu.VMEM((K, WIDE), F32),
            pltpu.VMEM((K, FT * TS - WIDE), F32),
            pltpu.VMEM((K, FT * TS - WIDE), F32),
            pltpu.VMEM((K, 4 * K), F32),
            pltpu.VMEM((COL - 1, K, 4 * K), F32),
            pltpu.VMEM((K, 4 * K), F32),
            pltpu.VMEM((K, 4 * K), F32),
            pltpu.SemaphoreType.DMA((3,)),
            pltpu.SemaphoreType.DMA((CHUNKS,)),
            pltpu.SemaphoreType.DMA((4,)),
            pltpu.SemaphoreType.DMA((4,)),
            pltpu.SemaphoreType.DMA((COL - 1,)),
            pltpu.SemaphoreType.DMA((COL - 1,)),
            pltpu.SemaphoreType.DMA,
            pltpu.SemaphoreType.DMA,
        ],
        compiler_params=pltpu.CompilerParams(
            collective_id=0, has_side_effects=True, vmem_limit_bytes=48 * 2**20
        ),
    )(defl, diag, vals, cols, west, north)


def exact(left, right):
    return jnp.dot(left, right, precision=HIGHEST, preferred_element_type=F32)


def exact_nt(left, right):
    return lax.dot_general(left, right, NT_DIMS, precision=HIGHEST, preferred_element_type=F32)


PANEL = 8


def inverse(packs):
    shape = (K, 4 * K)
    lane = lax.broadcasted_iota(jnp.int32, shape, 1)
    sub = lax.broadcasted_iota(jnp.int32, shape, 0)
    base = lane - lax.rem(lane, K)
    within = lax.rem(lane, K)
    packs = list(packs)
    for first in range(0, K, PANEL):
        panels = [
            [jnp.take_along_axis(m, base + (first + q), axis=1) for q in range(PANEL)]
            for m in packs
        ]
        for q in range(PANEL):
            k = first + q
            is_row = sub == k
            is_lane = within == k
            for at, m in enumerate(packs):
                panel = panels[at]
                column = panel[q]
                scale = 1.0 / column[k : k + 1]
                for later in range(q + 1, PANEL):
                    part = panel[later][k : k + 1] * scale
                    panel[later] = jnp.where(is_row, part, panel[later] - column * part)
                line = jnp.where(is_lane[0:1], 1.0, m[k : k + 1]) * scale
                packs[at] = jnp.where(is_row, line, jnp.where(is_lane, 0.0, m) - column * line)
    return packs


def chain_kernel(got_ref, coarse_ref, pivot_ref, mult_ref):
    col = lax.axis_index("gy")
    own = got_ref[COL - 1]
    self_own = own[:, 0:K]
    north_own = own[:, 3 * K : 4 * K]
    eye = (
        lax.broadcasted_iota(jnp.int32, (K, K), 0) == lax.broadcasted_iota(jnp.int32, (K, K), 1)
    ).astype(F32)
    nodes = {}
    links = {}
    for k in range(COL - 1):
        nodes[k] = jnp.where(k < col, got_ref[k][:, 0:K], eye)
    for k in range(COL - 2):
        link = got_ref[k][:, K : 2 * K] + got_ref[k + 1][:, 2 * K : 3 * K]
        link = jnp.where(k < col, link, 0.0)
        links[k] = (link, link.T)
    west_own = own[:, K : 2 * K] + got_ref[0][:, 2 * K : 3 * K]
    west_own = jnp.where(col > 0, west_own, 0.0)

    stride = 1
    while stride < COL - 1:
        gone = list(range(stride, COL - 1, 2 * stride))
        padded = gone + [gone[-1]] * (-len(gone) % 4)
        packs = [
            jnp.concatenate([nodes[k] for k in padded[at : at + 4]], axis=1)
            for at in range(0, len(padded), 4)
        ]
        packs = inverse(packs)
        fresh = {}
        for at, k in enumerate(gone):
            inv = packs[at // 4][:, (at % 4) * K : (at % 4 + 1) * K]
            near, near_t = links[k - stride]
            if k + stride < COL - 1:
                far, far_t = links[k]
                outer = exact(jnp.concatenate([near, far_t], axis=0), inv)
                to_near = exact_nt(outer, near)
                to_far = exact(outer, far)
                nodes[k - stride] = nodes[k - stride] - to_near[0:K]
                nodes[k + stride] = nodes[k + stride] - to_far[K : 2 * K]
                fresh[k - stride] = (-to_far[0:K], -to_near[K : 2 * K])
            else:
                nodes[k - stride] = nodes[k - stride] - exact_nt(exact(near, inv), near)
        links = fresh
        stride *= 2
    [pack] = inverse([jnp.concatenate([nodes[0]] * 4, axis=1)])
    mult = exact(west_own, pack[:, 0:K])
    pivot_ref[0, 0] = self_own - exact_nt(mult, west_own)
    mult_ref[0, 0] = mult
    coarse_ref[0, 0, 0] = self_own
    coarse_ref[0, 0, 1] = west_own
    coarse_ref[0, 0, 2] = north_own


def local(defl, diag, vals, cols, west, north):
    got = made_blocks(defl, diag, vals, cols, west, north)
    vmem = pl.BlockSpec(memory_space=pltpu.VMEM)
    return pl.pallas_call(
        chain_kernel,
        out_shape=(
            jax.ShapeDtypeStruct((1, 1, 3, K, K), F32),
            jax.ShapeDtypeStruct((1, 1, K, K), F32),
            jax.ShapeDtypeStruct((1, 1, K, K), F32),
        ),
        in_specs=[vmem],
        out_specs=(vmem, vmem, vmem),
        compiler_params=pltpu.CompilerParams(vmem_limit_bytes=16 * 2**20),
    )(got)


def solution(mesh):
    placed = (
        P("gx", "gy", None, None),
        P("gx", "gy", None),
        P("gx", "gy", None, None, None, None),
        P("gx", "gy", None, None),
        P("gx", "gy", None, None, None),
        P("gx", "gy", None, None, None),
    )
    return jax.shard_map(
        local,
        mesh=mesh,
        in_specs=placed,
        out_specs=(
            P("gx", "gy", None, None, None),
            P("gx", "gy", None, None),
            P("gx", "gy", None, None),
        ),
        check_vma=False,
    )
```

time: 270 us -> 50.5 us (0.19)
  other arithmetic: 101 us -> 0 us
  waiting for transfers between devices: 85.5 us -> 0 us
  Pallas kernels: 0 us -> 43.9 us
  starting transfers between devices: 36.1 us -> 0 us
  matrix products: 31.7 us -> 0 us
  local copies, waits for them, and re-layouts: 13.3 us -> 5.66 us
    another operation x75 -> x0, other arithmetic: 100 us -> none  [the longest x45 53.9 us: schur_step(): factor = jnp.linalg.cholesky(previous)]
    ppermute x17 -> x0, waiting for transfers between devices: 85.5 us -> none  [passed_along(): lax.ppermute(value, axis, [(source, source + steps) for source in range(f...]
    pallas_call x0 -> x2, Pallas kernels: none -> 43.9 us  [the longest x1 33.7 us: made_blocks(): pl.pallas_call(blocks_kernel, out_shape=jax.ShapeDtypeStruct((COL, K, 4 *...]
    ppermute x17 -> x0, starting transfers between devices: 36.1 us -> none  [passed_along(): lax.ppermute(value, axis, [(source, source + steps) for source in range(f...]
    dot_general x22 -> x0, matrix products: 26.1 us -> none  [the longest x1 7.77 us: local(): jnp.einsum('krs,rjst->rjkt', rounded, tile_vals[0, 0], preferred_element_...]
    another operation x30 -> x0, matrix products: 5.56 us -> none  [schur_step(): solved = jax.scipy.linalg.cho_solve((factor, True), low_block.T)]
    gather x1 -> x0, local copies, waits for them, and re-layouts: 2.98 us -> none  [local(): partners = vector_tiles[:, tile_cols[0, 0]]]
    unnamed x17 -> x9, local copies, waits for them, and re-layouts: 4.01 us -> 5.66 us
  transfers between devices with their start and end apart: 17 -> 0, of which waited for: 15 -> 0; matrix products, arithmetic and copies ran while one was open for 52% -> 0% of each run, Pallas kernels for 0% -> 0%
where the time goes in v1:
time: 50.5 us; the launch traced here: 50.2 us
  Pallas kernels  43.9 us (87%)
  local copies, waits for them, and re-layouts  5.66 us (11%)
  between operations  0.65 us (1%)
    pallas_call x1, Pallas kernels, made_blocks(): pl.pallas_call(blocks_kernel, out_shape=jax.ShapeDtypeStruct((COL, K, 4 *...  33.7 us
    pallas_call x1, Pallas kernels, local(): pl.pallas_call(chain_kernel, out_shape=(jax.ShapeDtypeStruct((1, 1, 3, K,...  10.2 us
    unnamed x9, local copies, waits for them, and re-layouts  5.66 us

profile of v1, /device:TPU:6, one launch (start us, length us, event | category | flops | bytes accessed | tf_op | source)
XLA Modules:
  0.0 50.2 jit_solution(10319296163491662398)
XLA Ops:
  0.6 0.8 %copy.9.cols_ref = s32[1,1,128,2]{3,2,1,0:T(8,128)S(1)} copy(s32[1,1,128,2]{2,3,1,0:T(2,128)} %param.9) | data formatting | bytes 2048 | tf_op args[3]
  1.4 0.0 copy-start
  1.4 1.6 %copy-done = f32[1,1,32,16384]{3,2,1,0:T(8,128)S(1)} copy-done((f32[1,1,32,16384]{3,2,1,0:T(8,128)S(1)}, f32[1,1,32,16384]{3,2,1,0:T(8,128)}, u32[]{:S(2)}) %copy-start) | copy-done | bytes 2097176
  3.0 0.0 copy-start.1
  3.0 1.2 %copy-done.1 = bf16[1,1,32,128,128]{4,3,2,1,0:T(8,128)(2,1)S(1)} copy-done((bf16[1,1,32,128,128]{4,3,2,1,0:T(8,128)(2,1)S(1)}, bf16[1,1,32,128,128]{4,3,2,1,0:T(8,128)(2,1)}, u32[]{:S(2)}) %copy-start.1) | copy-done | bytes 1048600
  4.2 0.0 copy-start.2
  4.2 1.2 %copy-done.2 = bf16[1,1,32,128,128]{4,3,2,1,0:T(8,128)(2,1)S(1)} copy-done((bf16[1,1,32,128,128]{4,3,2,1,0:T(8,128)(2,1)S(1)}, bf16[1,1,32,128,128]{4,3,2,1,0:T(8,128)(2,1)}, u32[]{:S(2)}) %copy-start.2) | copy-done | bytes 1048600
  5.5 0.0 copy-start.3
  5.5 0.8 %copy-done.3 = f32[1,1,16384]{2,1,0:T(1,128)S(1)} copy-done((f32[1,1,16384]{2,1,0:T(1,128)S(1)}, f32[1,1,16384]{2,1,0:T(1,128)}, u32[]{:S(2)}) %copy-start.3) | copy-done | bytes 65560
  6.3 33.7 %shard_map.85.got_ref = f32[16,32,128]{2,1,0:T(8,128)S(1)} custom-call(f32[1,1,32,16384]{3,2,1,0:T(8,128)S(1)} %copy-done, f32[1,1,16384]{2,1,0:T(1,128)S(1)} %copy-done.3, bf16[1,1,128,2,128,128]{5,4,3,2,1,0:T(8,128)(2,1)} %vals_hbm.1, s32[1,1,128,2]{3,2,1,0:T(8,128)S(1)} %copy.9.cols_ref, bf16[1,1,32,128,128]{4,3,2,1,0:T(8,128)(2,1)S(1)} %copy-done.1, ...), custom_call_target="tpu_custom_call" | custom-call | tf_op jit(solution)/shard_map/pallas_call | solution.py:216
  40.0 10.2 %shard_map.86 = (f32[1,1,3,32,32]{4,3,2,1,0:T(8,128)}, f32[1,1,32,32]{3,2,1,0:T(8,128)}, f32[1,1,32,32]{3,2,1,0:T(8,128)}) custom-call(f32[16,32,128]{2,1,0:T(8,128)S(1)} %shard_map.85.got_ref), custom_call_target="tpu_custom_call" | custom-call | tf_op jit(solution)/shard_map/pallas_call | solution.py:347
Async XLA Ops:
  1.4 1.6 %copy-start = (f32[1,1,32,16384]{3,2,1,0:T(8,128)S(1)}, f32[1,1,32,16384]{3,2,1,0:T(8,128)}, u32[]{:S(2)}) copy-start(f32[1,1,32,16384]{3,2,1,0:T(8,128)} %defl_hbm.1) | copy-start | bytes 6291460
  3.0 1.2 %copy-start.1 = (bf16[1,1,32,128,128]{4,3,2,1,0:T(8,128)(2,1)S(1)}, bf16[1,1,32,128,128]{4,3,2,1,0:T(8,128)(2,1)}, u32[]{:S(2)}) copy-start(bf16[1,1,32,128,128]{4,3,2,1,0:T(8,128)(2,1)} %west_hbm.1) | copy-start | bytes 3145732
  4.2 1.2 %copy-start.2 = (bf16[1,1,32,128,128]{4,3,2,1,0:T(8,128)(2,1)S(1)}, bf16[1,1,32,128,128]{4,3,2,1,0:T(8,128)(2,1)}, u32[]{:S(2)}) copy-start(bf16[1,1,32,128,128]{4,3,2,1,0:T(8,128)(2,1)} %north_hbm.1) | copy-start | bytes 3145732
  5.5 0.8 %copy-start.3 = (f32[1,1,16384]{2,1,0:T(1,128)S(1)}, f32[1,1,16384]{2,1,0:T(1,128)}, u32[]{:S(2)}) copy-start(f32[1,1,16384]{2,1,0:T(1,128)} %diag_ref.1) | copy-start | bytes 196612

commit v2 on v1

--- a/solution.py
+++ b/solution.py
@@ -21,7 +21,7 @@
 COL = 16
 HALF = 16
 WIDE = HALF * TS
-CHUNKS = 16
+CHUNKS = 8
 PER = NT // CHUNKS
 NT_DIMS = (((1,), (1,)), ((), ()))
 
@@ -67,25 +67,35 @@
     load_vec.start()
     load_west.start()
     load_north.start()
-    load_vals = []
+
+    def load_vals(c):
+        part = pl.ds(c * PER, PER)
+        return pltpu.make_async_copy(vals_hbm.at[0, 0, part], vals.at[part], sem_vals.at[c])
+
     for c in range(CHUNKS):
-        part = pl.ds(c * PER, PER)
-        load_vals.append(
-            pltpu.make_async_copy(vals_hbm.at[0, 0, part], vals.at[part], sem_vals.at[c])
-        )
-        load_vals[-1].start()
+        load_vals(c).start()
 
     barrier = pltpu.get_barrier_semaphore()
+    def greet(there, device):
+        @pl.when(there)
+        def _():
+            pl.semaphore_signal(barrier, inc=1, device_id=device, device_id_type=MESH)
+
     for step in range(1, COL):
-        pl.semaphore_signal(
-            barrier, inc=1, device_id={"gy": lax.rem(col + step, COL)}, device_id_type=MESH
-        )
-    pl.semaphore_signal(barrier, inc=1, device_id=south, device_id_type=MESH)
-    pl.semaphore_signal(barrier, inc=1, device_id=north_of, device_id_type=MESH)
-    pl.semaphore_wait(barrier, COL + 1)
+        greet(col >= step, {"gy": lax.rem(col + COL - step, COL)})
+    greet(col < COL - 1, east)
+    greet(row < ROW - 1, south)
+    greet(row > 0, north_of)
+    partners = (
+        (COL - 1 - col)
+        + jnp.where(col > 0, 1, 0)
+        + jnp.where(row < ROW - 1, 1, 0)
+        + jnp.where(row > 0, 1, 0)
+    )
+    pl.semaphore_wait(barrier, partners)
 
     def remote(source, target, at, device):
-        copy = pltpu.make_async_remote_copy(
+        return pltpu.make_async_remote_copy(
             src_ref=source,
             dst_ref=target,
             send_sem=send_band.at[at],
@@ -93,11 +103,13 @@
             device_id=device,
             device_id_type=MESH,
         )
-        copy.start()
-        return copy
 
     move_e = remote(defl_hbm.at[0, 0, :, pl.ds(FT * TS, WIDE)], got_e, 0, east)
     move_s = remote(defl_hbm.at[0, 0, :, pl.ds(3 * FT * TS, WIDE)], got_s, 1, south)
+    move_pw = remote(proj_w.at[:, pl.ds(WIDE, FT * TS - WIDE)], got_pw, 2, west_of)
+    move_pn = remote(proj_n.at[:, pl.ds(WIDE, FT * TS - WIDE)], got_pn, 3, north_of)
+    pl.when(col < COL - 1)(move_e.start)
+    pl.when(row < ROW - 1)(move_s.start)
 
     load_vec.wait()
 
@@ -110,7 +122,7 @@
         scaled = stacked(values * (diag_ref[0, :, part] * 0.5))
         return total + nt_dot(scaled, both)
 
-    total = lax.fori_loop(0, NL // 1024, split, jnp.zeros((2 * K, 2 * K), F32))
+    total = lax.fori_loop(0, NL // 1024, split, jnp.zeros((2 * K, 2 * K), F32), unroll=4)
 
     def project(tiles, first, target):
         def one(f, carry):
@@ -124,24 +136,24 @@
 
     load_west.wait()
     lax.fori_loop(HALF, FT, project(west, 0, proj_w), 0, unroll=4)
-    move_pw = remote(proj_w.at[:, pl.ds(WIDE, FT * TS - WIDE)], got_pw, 2, west_of)
+    pl.when(col > 0)(move_pw.start)
     load_north.wait()
     lax.fori_loop(HALF, FT, project(north, 2 * FT, proj_n), 0, unroll=4)
-    move_pn = remote(proj_n.at[:, pl.ds(WIDE, FT * TS - WIDE)], got_pn, 3, north_of)
+    pl.when(row > 0)(move_pn.start)
     lax.fori_loop(0, HALF, project(west, 0, proj_w), 0, unroll=4)
     lax.fori_loop(0, HALF, project(north, 2 * FT, proj_n), 0, unroll=4)
 
-    def tile_row(r, total):
-        own = pair[r, 0:K]
-        left, right = [], []
-        for j in range(2):
-            left.append(stacked(jnp.dot(own, vals[r, j], preferred_element_type=F32)))
-            right.append(pair[cols_ref[0, 0, r, j]])
-        return total + nt_dot(jnp.concatenate(left, axis=1), jnp.concatenate(right, axis=1))
-
-    for c in range(CHUNKS):
-        load_vals[c].wait()
-        total = lax.fori_loop(c * PER, (c + 1) * PER, tile_row, total, unroll=8)
+    def tile_rows(c, total):
+        load_vals(c).wait()
+        for i in range(PER):
+            r = c * PER + i
+            tiles = jnp.concatenate([vals[r, 0], vals[r, 1]], axis=1)
+            left = jnp.dot(pair[r, 0:K], tiles, preferred_element_type=F32)
+            right = jnp.concatenate([pair[cols_ref[0, 0, j, r]] for j in range(2)], axis=1)
+            total = total + nt_dot(stacked(left), right)
+        return total
+
+    total = lax.fori_loop(0, CHUNKS, tile_rows, total)
     cross = folded(total)
     self_block = cross + cross.T
 
@@ -153,17 +165,17 @@
 
         return -folded(lax.fori_loop(0, count // 512, one, jnp.zeros((2 * K, 2 * K), F32)))
 
-    move_e.wait_recv()
+    pl.when(col > 0)(move_e.wait_recv)
     west_here = jnp.where(col > 0, band(proj_w, 0, got_e, 0, WIDE), 0.0)
-    move_pw.wait_recv()
+    pl.when(col < COL - 1)(move_pw.wait_recv)
     west_next = band(got_pw, 0, vec, FT * TS + WIDE, FT * TS - WIDE)
-    move_pn.wait_recv()
+    pl.when(row < ROW - 1)(move_pn.wait_recv)
     sent_n[:, 0:K] = band(got_pn, 0, vec, 3 * FT * TS + WIDE, FT * TS - WIDE)
     move_n = pltpu.make_async_remote_copy(
         src_ref=sent_n, dst_ref=got_n, send_sem=send_n, recv_sem=recv_n,
         device_id=south, device_id_type=MESH,
     )
-    move_n.start()
+    pl.when(row < ROW - 1)(move_n.start)
     mine[...] = jnp.concatenate([self_block, west_here, west_next, west_next], axis=1)
 
     def to_row(step):
@@ -181,9 +193,9 @@
         def _():
             to_row(step).start()
 
-    move_s.wait_recv()
+    pl.when(row > 0)(move_s.wait_recv)
     north_here = band(proj_n, 0, got_s, 0, WIDE)
-    move_n.wait_recv()
+    pl.when(row > 0)(move_n.wait_recv)
     north_block = jnp.where(row > 0, north_here + got_n[:, 0:K], 0.0)
     out_ref[COL - 1] = jnp.concatenate(
         [self_block, west_here, west_next, north_block], axis=1
@@ -203,11 +215,11 @@
         def _():
             to_row(step).wait_send()
 
-    move_e.wait_send()
-    move_s.wait_send()
-    move_pw.wait_send()
-    move_pn.wait_send()
-    move_n.wait_send()
+    pl.when(col < COL - 1)(move_e.wait_send)
+    pl.when(row < ROW - 1)(move_s.wait_send)
+    pl.when(col > 0)(move_pw.wait_send)
+    pl.when(row > 0)(move_pn.wait_send)
+    pl.when(row < ROW - 1)(move_n.wait_send)
 
 
 def made_blocks(defl, diag, vals, cols, west, north):
@@ -244,7 +256,7 @@
             pltpu.SemaphoreType.DMA,
         ],
         compiler_params=pltpu.CompilerParams(
-            collective_id=0, has_side_effects=True, vmem_limit_bytes=48 * 2**20
+            collective_id=0, has_side_effects=True, vmem_limit_bytes=60 * 2**20
         ),
     )(defl, diag, vals, cols, west, north)
 
@@ -257,22 +269,19 @@
     return lax.dot_general(left, right, NT_DIMS, precision=HIGHEST, preferred_element_type=F32)
 
 
-PANEL = 8
-
-
-def inverse(packs):
+def inverse(packs, width):
     shape = (K, 4 * K)
     lane = lax.broadcasted_iota(jnp.int32, shape, 1)
     sub = lax.broadcasted_iota(jnp.int32, shape, 0)
-    base = lane - lax.rem(lane, K)
     within = lax.rem(lane, K)
+    base = lane - within
     packs = list(packs)
-    for first in range(0, K, PANEL):
+    for first in range(0, K, width):
         panels = [
-            [jnp.take_along_axis(m, base + (first + q), axis=1) for q in range(PANEL)]
+            [jnp.take_along_axis(m, base + (first + q), axis=1) for q in range(width)]
             for m in packs
         ]
-        for q in range(PANEL):
+        for q in range(width):
             k = first + q
             is_row = sub == k
             is_lane = within == k
@@ -280,7 +289,7 @@
                 panel = panels[at]
                 column = panel[q]
                 scale = 1.0 / column[k : k + 1]
-                for later in range(q + 1, PANEL):
+                for later in range(q + 1, width):
                     part = panel[later][k : k + 1] * scale
                     panel[later] = jnp.where(is_row, part, panel[later] - column * part)
                 line = jnp.where(is_lane[0:1], 1.0, m[k : k + 1]) * scale
@@ -288,61 +297,72 @@
     return packs
 
 
-def chain_kernel(got_ref, coarse_ref, pivot_ref, mult_ref):
+NODES = COL - 1
+
+
+def chain_kernel(got_ref, coarse_ref, pivot_ref, mult_ref, nodes, links, turned):
     col = lax.axis_index("gy")
     own = got_ref[COL - 1]
     self_own = own[:, 0:K]
-    north_own = own[:, 3 * K : 4 * K]
+    west_own = own[:, K : 2 * K] + got_ref[0][:, 2 * K : 3 * K]
+    west_own = jnp.where(col > 0, west_own, 0.0)
+    coarse_ref[0, 0, 0] = self_own
+    coarse_ref[0, 0, 1] = west_own
+    coarse_ref[0, 0, 2] = own[:, 3 * K : 4 * K]
     eye = (
         lax.broadcasted_iota(jnp.int32, (K, K), 0) == lax.broadcasted_iota(jnp.int32, (K, K), 1)
     ).astype(F32)
-    nodes = {}
-    links = {}
-    for k in range(COL - 1):
-        nodes[k] = jnp.where(k < col, got_ref[k][:, 0:K], eye)
-    for k in range(COL - 2):
-        link = got_ref[k][:, K : 2 * K] + got_ref[k + 1][:, 2 * K : 3 * K]
-        link = jnp.where(k < col, link, 0.0)
-        links[k] = (link, link.T)
-    west_own = own[:, K : 2 * K] + got_ref[0][:, 2 * K : 3 * K]
-    west_own = jnp.where(col > 0, west_own, 0.0)
-
-    stride = 1
-    while stride < COL - 1:
-        gone = list(range(stride, COL - 1, 2 * stride))
-        padded = gone + [gone[-1]] * (-len(gone) % 4)
-        packs = [
-            jnp.concatenate([nodes[k] for k in padded[at : at + 4]], axis=1)
-            for at in range(0, len(padded), 4)
-        ]
-        packs = inverse(packs)
-        fresh = {}
+    nodes[0] = jnp.where(col > 0, got_ref[0][:, 0:K], eye)
+
+    def level(stride):
+        if stride == 1:
+            held, fresh_links = {}, {}
+            for k in range(NODES):
+                held[k] = jnp.where(k < col, got_ref[k][:, 0:K], eye)
+            for k in range(NODES - 1):
+                link = got_ref[k][:, K : 2 * K] + got_ref[k + 1][:, 2 * K : 3 * K]
+                link = jnp.where(k < col, link, 0.0)
+                fresh_links[k] = (link, link.T)
+        else:
+            held = {k: nodes[k] for k in range(0, NODES, stride)}
+            fresh_links = {k: (links[k], turned[k]) for k in range(0, NODES - stride, stride)}
+        gone = list(range(stride, NODES, 2 * stride))
+        if len(gone) == 1:
+            packs = [jnp.concatenate([held[gone[0]]] * 4, axis=1)]
+        else:
+            padded = gone + [gone[-1]] * (-len(gone) % 4)
+            packs = [
+                jnp.concatenate([held[k] for k in padded[at : at + 4]], axis=1)
+                for at in range(0, len(padded), 4)
+            ]
+        packs = inverse(packs, 8 if len(packs) > 1 else 16)
         for at, k in enumerate(gone):
             inv = packs[at // 4][:, (at % 4) * K : (at % 4 + 1) * K]
-            near, near_t = links[k - stride]
-            if k + stride < COL - 1:
-                far, far_t = links[k]
+            near, near_t = fresh_links[k - stride]
+            if k + stride < NODES:
+                far, far_t = fresh_links[k]
                 outer = exact(jnp.concatenate([near, far_t], axis=0), inv)
                 to_near = exact_nt(outer, near)
                 to_far = exact(outer, far)
-                nodes[k - stride] = nodes[k - stride] - to_near[0:K]
-                nodes[k + stride] = nodes[k + stride] - to_far[K : 2 * K]
-                fresh[k - stride] = (-to_far[0:K], -to_near[K : 2 * K])
+                held[k - stride] = held[k - stride] - to_near[0:K]
+                held[k + stride] = held[k + stride] - to_far[K : 2 * K]
+                links[k - stride] = -to_far[0:K]
+                turned[k - stride] = -to_near[K : 2 * K]
             else:
-                nodes[k - stride] = nodes[k - stride] - exact_nt(exact(near, inv), near)
-        links = fresh
-        stride *= 2
-    [pack] = inverse([jnp.concatenate([nodes[0]] * 4, axis=1)])
+                held[k - stride] = held[k - stride] - exact_nt(exact(near, inv), near)
+        for k in range(0, NODES, 2 * stride):
+            nodes[k] = held[k]
+
+    for stride in (1, 2, 4, 8):
+        pl.when(col > stride)(functools.partial(level, stride))
+    [pack] = inverse([jnp.concatenate([nodes[0]] * 4, axis=1)], 16)
     mult = exact(west_own, pack[:, 0:K])
     pivot_ref[0, 0] = self_own - exact_nt(mult, west_own)
     mult_ref[0, 0] = mult
-    coarse_ref[0, 0, 0] = self_own
-    coarse_ref[0, 0, 1] = west_own
-    coarse_ref[0, 0, 2] = north_own
 
 
 def local(defl, diag, vals, cols, west, north):
-    got = made_blocks(defl, diag, vals, cols, west, north)
+    got = made_blocks(defl, diag, vals, jnp.swapaxes(cols, 2, 3), west, north)
     vmem = pl.BlockSpec(memory_space=pltpu.VMEM)
     return pl.pallas_call(
         chain_kernel,
@@ -353,6 +373,7 @@
         ),
         in_specs=[vmem],
         out_specs=(vmem, vmem, vmem),
+        scratch_shapes=[pltpu.VMEM((NODES, K, K), F32)] * 3,
         compiler_params=pltpu.CompilerParams(vmem_limit_bytes=16 * 2**20),
     )(got)
 

time: 50.5 us -> 34 us (0.67)
  Pallas kernels: 43.9 us -> 32.2 us
  local copies, waits for them, and re-layouts: 5.66 us -> 0.94 us
    pallas_call x1, Pallas kernels: 33.7 us -> 22.7 us  [made_blocks(): pl.pallas_call(blocks_kernel, out_shape=jax.ShapeDtypeStruct((COL, K, 4 *...]
    unnamed x9 -> x2, local copies, waits for them, and re-layouts: 5.66 us -> 0.94 us
    pallas_call x1, Pallas kernels: 10.2 us -> 9.52 us  [local(): pl.pallas_call(chain_kernel, out_shape=(jax.ShapeDtypeStruct((1, 1, 3, K,...]
where the time goes in v2:
time: 34 us; the launch traced here: 33.8 us
  Pallas kernels  32.2 us (95%)
  local copies, waits for them, and re-layouts  0.94 us (3%)
  between operations  0.65 us (2%)
    pallas_call x1, Pallas kernels, made_blocks(): pl.pallas_call(blocks_kernel, out_shape=jax.ShapeDtypeStruct((COL, K, 4 *...  22.7 us
    pallas_call x1, Pallas kernels, local(): pl.pallas_call(chain_kernel, out_shape=(jax.ShapeDtypeStruct((1, 1, 3, K,...  9.52 us
    unnamed x2, local copies, waits for them, and re-layouts  0.94 us

profile of v2, /device:TPU:6, one launch (start us, length us, event | category | flops | bytes accessed | tf_op | source)
XLA Modules:
  0.0 33.8 jit_solution(15097531094243386654)
XLA Ops:
  0.6 22.7 %shard_map.85.got_ref = f32[16,32,128]{2,1,0:T(8,128)} custom-call(f32[1,1,32,16384]{3,2,1,0:T(8,128)} %defl_hbm.1, f32[1,1,16384]{2,1,0:T(1,128)} %diag_ref.1, bf16[1,1,128,2,128,128]{5,4,3,2,1,0:T(8,128)(2,1)} %vals_hbm.1, s32[1,1,2,128]{3,2,1,0:T(2,128)} %bitcast.1, bf16[1,1,32,128,128]{4,3,2,1,0:T(8,128)(2,1)} %west_hbm.1, ...), custom_call_target="tpu_custom_call" | custom-call | tf_op jit(solution)/shard_map/pallas_call | solution.py:228
  23.3 0.0 copy-start
  23.4 0.9 %copy-done = f32[16,32,128]{2,1,0:T(8,128)S(1)} copy-done((f32[16,32,128]{2,1,0:T(8,128)S(1)}, f32[16,32,128]{2,1,0:T(8,128)}, u32[]{:S(2)}) %copy-start) | copy-done | bytes 262168
  24.3 9.5 %shard_map.86 = (f32[1,1,3,32,32]{4,3,2,1,0:T(8,128)}, f32[1,1,32,32]{3,2,1,0:T(8,128)}, f32[1,1,32,32]{3,2,1,0:T(8,128)}) custom-call(f32[16,32,128]{2,1,0:T(8,128)S(1)} %copy-done), custom_call_target="tpu_custom_call" | custom-call | tf_op jit(solution)/shard_map/pallas_call | solution.py:367
Async XLA Ops:
  23.3 1.0 %copy-start = (f32[16,32,128]{2,1,0:T(8,128)S(1)}, f32[16,32,128]{2,1,0:T(8,128)}, u32[]{:S(2)}) copy-start(f32[16,32,128]{2,1,0:T(8,128)} %shard_map.85.got_ref) | copy-start | bytes 786436

commit v3 on v2

--- a/solution.py
+++ b/solution.py
@@ -47,10 +47,43 @@
     return lax.dot_general(left, right, NT_DIMS, preferred_element_type=F32)
 
 
+def exact(left, right):
+    return jnp.dot(left, right, precision=HIGHEST, preferred_element_type=F32)
+
+
+def exact_nt(left, right):
+    return lax.dot_general(left, right, NT_DIMS, precision=HIGHEST, preferred_element_type=F32)
+
+
+def inverses(blocks, width):
+    lane = lax.broadcasted_iota(jnp.int32, (K, K), 1)
+    sub = lax.broadcasted_iota(jnp.int32, (K, K), 0)
+    blocks = list(blocks)
+    for first in range(0, K, width):
+        panels = [
+            [jnp.broadcast_to(m[:, first + q : first + q + 1], (K, K)) for q in range(width)]
+            for m in blocks
+        ]
+        for q in range(width):
+            k = first + q
+            is_row = sub == k
+            is_lane = lane == k
+            for at, m in enumerate(blocks):
+                panel = panels[at]
+                column = panel[q]
+                scale = 1.0 / column[k : k + 1]
+                for later in range(q + 1, width):
+                    part = panel[later][k : k + 1] * scale
+                    panel[later] = jnp.where(is_row, part, panel[later] - column * part)
+                line = jnp.where(is_lane[0:1], 1.0, m[k : k + 1]) * scale
+                blocks[at] = jnp.where(is_row, line, jnp.where(is_lane, 0.0, m) - column * line)
+    return blocks
+
+
 def blocks_kernel(
     defl_hbm, diag_ref, vals_hbm, cols_ref, west_hbm, north_hbm,
     out_ref,
-    vec, pair, vals, west, north, proj_w, proj_n,
+    vec, pair, vals, west, north, here_w, here_n, proj_w, proj_n,
     got_e, got_s, got_pw, got_pn, mine, slots, got_n, sent_n,
     sem_in, sem_vals, send_band, recv_band, send_row, recv_row, send_n, recv_n,
 ):
@@ -68,14 +101,8 @@
     load_west.start()
     load_north.start()
 
-    def load_vals(c):
-        part = pl.ds(c * PER, PER)
-        return pltpu.make_async_copy(vals_hbm.at[0, 0, part], vals.at[part], sem_vals.at[c])
-
-    for c in range(CHUNKS):
-        load_vals(c).start()
-
     barrier = pltpu.get_barrier_semaphore()
+
     def greet(there, device):
         @pl.when(there)
         def _():
@@ -92,6 +119,53 @@
         + jnp.where(row < ROW - 1, 1, 0)
         + jnp.where(row > 0, 1, 0)
     )
+
+    def load_vals(c):
+        part = pl.ds(c * PER, PER)
+        return pltpu.make_async_copy(vals_hbm.at[0, 0, part], vals.at[part], sem_vals.at[c])
+
+    load_vec.wait()
+    for c in range(CHUNKS):
+        load_vals(c).start()
+
+    def split(c, total):
+        part = pl.ds(pl.multiple_of(c * 1024, 1024), 1024)
+        values = vec[:, part]
+        both = stacked(values)
+        for t in range(8):
+            pair[c * 8 + t] = both[:, t * TS : (t + 1) * TS]
+        scaled = stacked(values * (diag_ref[0, :, part] * 0.5))
+        return total + nt_dot(scaled, both)
+
+    def project(tiles, first, f):
+        return jnp.dot(pair[first + f, 0:K], tiles[f], preferred_element_type=F32)
+
+    def send_off(tiles, first, target):
+        def one(q, carry):
+            made = [project(tiles, first, HALF + q * 4 + i) for i in range(4)]
+            target[:, pl.ds(pl.multiple_of(q * 4 * TS, 4 * TS), 4 * TS)] = jnp.concatenate(made, axis=1)
+            return carry
+
+        lax.fori_loop(0, (FT - HALF) // 4, one, 0, unroll=2)
+
+    def keep(tiles, first, target):
+        def one(q, carry):
+            made = [project(tiles, first, q * 4 + i) for i in range(4)]
+            target[:, pl.ds(pl.multiple_of(q * 4 * TS, 4 * TS), 4 * TS)] = stacked(
+                jnp.concatenate(made, axis=1)
+            )
+            return carry
+
+        lax.fori_loop(0, HALF // 4, one, 0, unroll=2)
+
+    total = jnp.zeros((2 * K, 2 * K), F32)
+    total = lax.fori_loop(2, 4, split, total, unroll=2)
+    total = lax.fori_loop(10, 12, split, total, unroll=2)
+    load_west.wait()
+    send_off(west, 0, proj_w)
+    load_north.wait()
+    send_off(north, 2 * FT, proj_n)
+
     pl.semaphore_wait(barrier, partners)
 
     def remote(source, target, at, device):
@@ -104,44 +178,20 @@
             device_id_type=MESH,
         )
 
-    move_e = remote(defl_hbm.at[0, 0, :, pl.ds(FT * TS, WIDE)], got_e, 0, east)
-    move_s = remote(defl_hbm.at[0, 0, :, pl.ds(3 * FT * TS, WIDE)], got_s, 1, south)
-    move_pw = remote(proj_w.at[:, pl.ds(WIDE, FT * TS - WIDE)], got_pw, 2, west_of)
-    move_pn = remote(proj_n.at[:, pl.ds(WIDE, FT * TS - WIDE)], got_pn, 3, north_of)
+    move_e = remote(vec.at[:, pl.ds(FT * TS, WIDE)], got_e, 0, east)
+    move_s = remote(vec.at[:, pl.ds(3 * FT * TS, WIDE)], got_s, 1, south)
+    move_pw = remote(proj_w, got_pw, 2, west_of)
+    move_pn = remote(proj_n, got_pn, 3, north_of)
     pl.when(col < COL - 1)(move_e.start)
+    pl.when(col > 0)(move_pw.start)
     pl.when(row < ROW - 1)(move_s.start)
-
-    load_vec.wait()
-
-    def split(c, total):
-        part = pl.ds(pl.multiple_of(c * 1024, 1024), 1024)
-        values = vec[:, part]
-        both = stacked(values)
-        for t in range(8):
-            pair[c * 8 + t] = both[:, t * TS : (t + 1) * TS]
-        scaled = stacked(values * (diag_ref[0, :, part] * 0.5))
-        return total + nt_dot(scaled, both)
-
-    total = lax.fori_loop(0, NL // 1024, split, jnp.zeros((2 * K, 2 * K), F32), unroll=4)
-
-    def project(tiles, first, target):
-        def one(f, carry):
-            place = pl.ds(pl.multiple_of(f * TS, TS), TS)
-            target[:, place] = jnp.dot(
-                pair[first + f, 0:K], tiles[f], preferred_element_type=F32
-            )
-            return carry
-
-        return one
-
-    load_west.wait()
-    lax.fori_loop(HALF, FT, project(west, 0, proj_w), 0, unroll=4)
-    pl.when(col > 0)(move_pw.start)
-    load_north.wait()
-    lax.fori_loop(HALF, FT, project(north, 2 * FT, proj_n), 0, unroll=4)
     pl.when(row > 0)(move_pn.start)
-    lax.fori_loop(0, HALF, project(west, 0, proj_w), 0, unroll=4)
-    lax.fori_loop(0, HALF, project(north, 2 * FT, proj_n), 0, unroll=4)
+
+    total = lax.fori_loop(0, 2, split, total, unroll=2)
+    total = lax.fori_loop(4, 10, split, total, unroll=3)
+    total = lax.fori_loop(12, 16, split, total, unroll=4)
+    keep(west, 0, here_w)
+    keep(north, 2 * FT, here_n)
 
     def tile_rows(c, total):
         load_vals(c).wait()
@@ -156,31 +206,41 @@
     total = lax.fori_loop(0, CHUNKS, tile_rows, total)
     cross = folded(total)
     self_block = cross + cross.T
-
-    def band(left, left_at, right, right_at, count):
-        def one(c, acc):
-            a = left[:, pl.ds(pl.multiple_of(left_at + c * 512, 512), 512)]
-            b = right[:, pl.ds(pl.multiple_of(right_at + c * 512, 512), 512)]
-            return acc + nt_dot(stacked(a), stacked(b))
-
-        return -folded(lax.fori_loop(0, count // 512, one, jnp.zeros((2 * K, 2 * K), F32)))
+    [self_inverse] = inverses([self_block], 16)
+
+    zeros = jnp.zeros((2 * K, 2 * K), F32)
+
+    def here_band(left, right):
+        def one(c, sums):
+            part = pl.ds(pl.multiple_of(c * 512, 512), 512)
+            a = left[:, part]
+            b = stacked(right[:, part])
+            return sums[0] + nt_dot(a, b), sums[1] + nt_dot(b, a)
+
+        sums = lax.fori_loop(0, WIDE // 512, one, (zeros, zeros), unroll=2)
+        return -folded(sums[0]), -folded(sums[1])
+
+    def next_band(left, first):
+        def one(c, sums):
+            a = stacked(left[:, pl.ds(pl.multiple_of(c * 512, 512), 512)])
+            b = jnp.concatenate([pair[first + c * 4 + i] for i in range(4)], axis=1)
+            return sums[0] + nt_dot(a, b), sums[1] + nt_dot(b, a)
+
+        sums = lax.fori_loop(0, (FT * TS - WIDE) // 512, one, (zeros, zeros), unroll=2)
+        return -folded(sums[0]), -folded(sums[1])
 
     pl.when(col > 0)(move_e.wait_recv)
-    west_here = jnp.where(col > 0, band(proj_w, 0, got_e, 0, WIDE), 0.0)
+    west_here, west_here_t = here_band(here_w, got_e)
+    west_here = jnp.where(col > 0, west_here, 0.0)
+    west_here_t = jnp.where(col > 0, west_here_t, 0.0)
     pl.when(col < COL - 1)(move_pw.wait_recv)
-    west_next = band(got_pw, 0, vec, FT * TS + WIDE, FT * TS - WIDE)
-    pl.when(row < ROW - 1)(move_pn.wait_recv)
-    sent_n[:, 0:K] = band(got_pn, 0, vec, 3 * FT * TS + WIDE, FT * TS - WIDE)
-    move_n = pltpu.make_async_remote_copy(
-        src_ref=sent_n, dst_ref=got_n, send_sem=send_n, recv_sem=recv_n,
-        device_id=south, device_id_type=MESH,
-    )
-    pl.when(row < ROW - 1)(move_n.start)
-    mine[...] = jnp.concatenate([self_block, west_here, west_next, west_next], axis=1)
+    west_next, west_next_t = next_band(got_pw, FT + HALF)
+    mine[0] = jnp.concatenate([self_block, west_next, west_here, west_next_t], axis=1)
+    mine[1] = jnp.concatenate([self_inverse, west_here, west_next, west_here_t], axis=1)
 
     def to_row(step):
         return pltpu.make_async_remote_copy(
-            src_ref=mine,
+            src_ref=mine.at[(step - 1) % 2],
             dst_ref=slots.at[step - 1],
             send_sem=send_row.at[step - 1],
             recv_sem=recv_row.at[step - 1],
@@ -193,12 +253,20 @@
         def _():
             to_row(step).start()
 
+    pl.when(row < ROW - 1)(move_pn.wait_recv)
+    sent_n[:, 0:K] = next_band(got_pn, 3 * FT + HALF)[0]
+    move_n = pltpu.make_async_remote_copy(
+        src_ref=sent_n, dst_ref=got_n, send_sem=send_n, recv_sem=recv_n,
+        device_id=south, device_id_type=MESH,
+    )
+    pl.when(row < ROW - 1)(move_n.start)
+
     pl.when(row > 0)(move_s.wait_recv)
-    north_here = band(proj_n, 0, got_s, 0, WIDE)
+    north_here = here_band(here_n, got_s)[0]
     pl.when(row > 0)(move_n.wait_recv)
     north_block = jnp.where(row > 0, north_here + got_n[:, 0:K], 0.0)
     out_ref[COL - 1] = jnp.concatenate(
-        [self_block, west_here, west_next, north_block], axis=1
+        [self_block, west_here, north_block, jnp.zeros((K, K), F32)], axis=1
     )
 
     for step in range(1, COL):
@@ -236,13 +304,15 @@
             pltpu.VMEM((NT, 2, TS, TS), BF16),
             pltpu.VMEM((FT, TS, TS), BF16),
             pltpu.VMEM((FT, TS, TS), BF16),
-            pltpu.VMEM((K, FT * TS), F32),
-            pltpu.VMEM((K, FT * TS), F32),
+            pltpu.VMEM((2 * K, WIDE), BF16),
+            pltpu.VMEM((2 * K, WIDE), BF16),
+            pltpu.VMEM((K, FT * TS - WIDE), F32),
+            pltpu.VMEM((K, FT * TS - WIDE), F32),
             pltpu.VMEM((K, WIDE), F32),
             pltpu.VMEM((K, WIDE), F32),
             pltpu.VMEM((K, FT * TS - WIDE), F32),
             pltpu.VMEM((K, FT * TS - WIDE), F32),
-            pltpu.VMEM((K, 4 * K), F32),
+            pltpu.VMEM((2, K, 4 * K), F32),
             pltpu.VMEM((COL - 1, K, 4 * K), F32),
             pltpu.VMEM((K, 4 * K), F32),
             pltpu.VMEM((K, 4 * K), F32),
@@ -259,14 +329,6 @@
             collective_id=0, has_side_effects=True, vmem_limit_bytes=60 * 2**20
         ),
     )(defl, diag, vals, cols, west, north)
-
-
-def exact(left, right):
-    return jnp.dot(left, right, precision=HIGHEST, preferred_element_type=F32)
-
-
-def exact_nt(left, right):
-    return lax.dot_general(left, right, NT_DIMS, precision=HIGHEST, preferred_element_type=F32)
 
 
 def inverse(packs, width):
@@ -304,43 +366,21 @@
     col = lax.axis_index("gy")
     own = got_ref[COL - 1]
     self_own = own[:, 0:K]
-    west_own = own[:, K : 2 * K] + got_ref[0][:, 2 * K : 3 * K]
+    west_own = (own + got_ref[0])[:, K : 2 * K]
     west_own = jnp.where(col > 0, west_own, 0.0)
     coarse_ref[0, 0, 0] = self_own
     coarse_ref[0, 0, 1] = west_own
-    coarse_ref[0, 0, 2] = own[:, 3 * K : 4 * K]
+    coarse_ref[0, 0, 2] = own[:, 2 * K : 3 * K]
     eye = (
         lax.broadcasted_iota(jnp.int32, (K, K), 0) == lax.broadcasted_iota(jnp.int32, (K, K), 1)
     ).astype(F32)
     nodes[0] = jnp.where(col > 0, got_ref[0][:, 0:K], eye)
 
-    def level(stride):
-        if stride == 1:
-            held, fresh_links = {}, {}
-            for k in range(NODES):
-                held[k] = jnp.where(k < col, got_ref[k][:, 0:K], eye)
-            for k in range(NODES - 1):
-                link = got_ref[k][:, K : 2 * K] + got_ref[k + 1][:, 2 * K : 3 * K]
-                link = jnp.where(k < col, link, 0.0)
-                fresh_links[k] = (link, link.T)
-        else:
-            held = {k: nodes[k] for k in range(0, NODES, stride)}
-            fresh_links = {k: (links[k], turned[k]) for k in range(0, NODES - stride, stride)}
-        gone = list(range(stride, NODES, 2 * stride))
-        if len(gone) == 1:
-            packs = [jnp.concatenate([held[gone[0]]] * 4, axis=1)]
-        else:
-            padded = gone + [gone[-1]] * (-len(gone) % 4)
-            packs = [
-                jnp.concatenate([held[k] for k in padded[at : at + 4]], axis=1)
-                for at in range(0, len(padded), 4)
-            ]
-        packs = inverse(packs, 8 if len(packs) > 1 else 16)
-        for at, k in enumerate(gone):
-            inv = packs[at // 4][:, (at % 4) * K : (at % 4 + 1) * K]
-            near, near_t = fresh_links[k - stride]
+    def eliminate(stride, held, gone, links_now, solved):
+        for k, inv in zip(gone, solved, strict=True):
+            near = links_now[k - stride][0]
             if k + stride < NODES:
-                far, far_t = fresh_links[k]
+                far, far_t = links_now[k]
                 outer = exact(jnp.concatenate([near, far_t], axis=0), inv)
                 to_near = exact_nt(outer, near)
                 to_far = exact(outer, far)
@@ -353,10 +393,34 @@
         for k in range(0, NODES, 2 * stride):
             nodes[k] = held[k]
 
-    for stride in (1, 2, 4, 8):
+    @pl.when(col > 1)
+    def _():
+        held = {k: jnp.where(k < col, got_ref[k][:, 0:K], eye) for k in range(0, NODES, 2)}
+        links_now = {}
+        for k in range(NODES - 1):
+            both = got_ref[k] + got_ref[k + 1]
+            if k % 2:
+                links_now[k] = (both[:, K : 2 * K], both[:, 3 * K : 4 * K])
+            else:
+                links_now[k] = (both[:, 2 * K : 3 * K],)
+        gone = list(range(1, NODES, 2))
+        eliminate(1, held, gone, links_now, [got_ref[k][:, 0:K] for k in gone])
+
+    def level(stride):
+        held = {k: nodes[k] for k in range(0, NODES, stride)}
+        links_now = {k: (links[k], turned[k]) for k in range(0, NODES - stride, stride)}
+        gone = list(range(stride, NODES, 2 * stride))
+        if len(gone) == 4:
+            [pack] = inverse([jnp.concatenate([held[k] for k in gone], axis=1)], 16)
+            solved = [pack[:, at * K : (at + 1) * K] for at in range(4)]
+        else:
+            solved = inverses([held[k] for k in gone], 16)
+        eliminate(stride, held, gone, links_now, solved)
+
+    for stride in (2, 4, 8):
         pl.when(col > stride)(functools.partial(level, stride))
-    [pack] = inverse([jnp.concatenate([nodes[0]] * 4, axis=1)], 16)
-    mult = exact(west_own, pack[:, 0:K])
+    [last] = inverses([nodes[0]], 16)
+    mult = exact(west_own, last)
     pivot_ref[0, 0] = self_own - exact_nt(mult, west_own)
     mult_ref[0, 0] = mult
 

time: 34 us -> 29.7 us (0.87)
  Pallas kernels: 32.2 us -> 27.9 us
    pallas_call x1, Pallas kernels: 22.7 us -> 20.3 us  [made_blocks(): pl.pallas_call(blocks_kernel, out_shape=jax.ShapeDtypeStruct((COL, K, 4 *...]
    pallas_call x1, Pallas kernels: 9.52 us -> 7.66 us  [local(): pl.pallas_call(chain_kernel, out_shape=(jax.ShapeDtypeStruct((1, 1, 3, K,...]
where the time goes in v3:
time: 29.7 us; the launch traced here: 29.5 us
  Pallas kernels  27.9 us (94%)
  local copies, waits for them, and re-layouts  0.94 us (3%)
  between operations  0.65 us (2%)
    pallas_call x1, Pallas kernels, made_blocks(): pl.pallas_call(blocks_kernel, out_shape=jax.ShapeDtypeStruct((COL, K, 4 *...  20.3 us
    pallas_call x1, Pallas kernels, local(): pl.pallas_call(chain_kernel, out_shape=(jax.ShapeDtypeStruct((1, 1, 3, K,...  7.66 us
    unnamed x2, local copies, waits for them, and re-layouts  0.94 us

profile of v3, /device:TPU:6, one launch (start us, length us, event | category | flops | bytes accessed | tf_op | source)
XLA Modules:
  0.0 29.5 jit_solution(3359113953309690668)
XLA Ops:
  0.6 20.3 %shard_map.85.got_ref = f32[16,32,128]{2,1,0:T(8,128)} custom-call(f32[1,1,32,16384]{3,2,1,0:T(8,128)} %defl_hbm.1, f32[1,1,16384]{2,1,0:T(1,128)} %diag_ref.1, bf16[1,1,128,2,128,128]{5,4,3,2,1,0:T(8,128)(2,1)} %vals_hbm.1, s32[1,1,2,128]{3,2,1,0:T(2,128)} %bitcast.1, bf16[1,1,32,128,128]{4,3,2,1,0:T(8,128)(2,1)} %west_hbm.1, ...), custom_call_target="tpu_custom_call" | custom-call | tf_op jit(solution)/shard_map/pallas_call | solution.py:296
  20.9 0.0 copy-start
  20.9 0.9 %copy-done = f32[16,32,128]{2,1,0:T(8,128)S(1)} copy-done((f32[16,32,128]{2,1,0:T(8,128)S(1)}, f32[16,32,128]{2,1,0:T(8,128)}, u32[]{:S(2)}) %copy-start) | copy-done | bytes 262168
  21.9 7.7 %shard_map.86 = (f32[1,1,3,32,32]{4,3,2,1,0:T(8,128)}, f32[1,1,32,32]{3,2,1,0:T(8,128)}, f32[1,1,32,32]{3,2,1,0:T(8,128)}) custom-call(f32[16,32,128]{2,1,0:T(8,128)S(1)} %copy-done), custom_call_target="tpu_custom_call" | custom-call | tf_op jit(solution)/shard_map/pallas_call | solution.py:431
Async XLA Ops:
  20.9 1.0 %copy-start = (f32[16,32,128]{2,1,0:T(8,128)S(1)}, f32[16,32,128]{2,1,0:T(8,128)}, u32[]{:S(2)}) copy-start(f32[16,32,128]{2,1,0:T(8,128)} %shard_map.85.got_ref) | copy-start | bytes 786436

commit v4 on v3

--- a/solution.py
+++ b/solution.py
@@ -217,7 +217,7 @@
             b = stacked(right[:, part])
             return sums[0] + nt_dot(a, b), sums[1] + nt_dot(b, a)
 
-        sums = lax.fori_loop(0, WIDE // 512, one, (zeros, zeros), unroll=2)
+        sums = lax.fori_loop(0, WIDE // 512, one, (zeros, zeros), unroll=4)
         return -folded(sums[0]), -folded(sums[1])
 
     def next_band(left, first):
@@ -226,7 +226,7 @@
             b = jnp.concatenate([pair[first + c * 4 + i] for i in range(4)], axis=1)
             return sums[0] + nt_dot(a, b), sums[1] + nt_dot(b, a)
 
-        sums = lax.fori_loop(0, (FT * TS - WIDE) // 512, one, (zeros, zeros), unroll=2)
+        sums = lax.fori_loop(0, (FT * TS - WIDE) // 512, one, (zeros, zeros), unroll=4)
         return -folded(sums[0]), -folded(sums[1])
 
     pl.when(col > 0)(move_e.wait_recv)
@@ -295,7 +295,7 @@
     vmem = pl.BlockSpec(memory_space=pltpu.VMEM)
     return pl.pallas_call(
         blocks_kernel,
-        out_shape=jax.ShapeDtypeStruct((COL, K, 4 * K), F32),
+        out_shape=pltpu.VMEM((COL, K, 4 * K), F32),
         in_specs=[hbm, vmem, hbm, pl.BlockSpec(memory_space=pltpu.SMEM), hbm, hbm],
         out_specs=vmem,
         scratch_shapes=[
@@ -331,34 +331,6 @@
     )(defl, diag, vals, cols, west, north)
 
 
-def inverse(packs, width):
-    shape = (K, 4 * K)
-    lane = lax.broadcasted_iota(jnp.int32, shape, 1)
-    sub = lax.broadcasted_iota(jnp.int32, shape, 0)
-    within = lax.rem(lane, K)
-    base = lane - within
-    packs = list(packs)
-    for first in range(0, K, width):
-        panels = [
-            [jnp.take_along_axis(m, base + (first + q), axis=1) for q in range(width)]
-            for m in packs
-        ]
-        for q in range(width):
-            k = first + q
-            is_row = sub == k
-            is_lane = within == k
-            for at, m in enumerate(packs):
-                panel = panels[at]
-                column = panel[q]
-                scale = 1.0 / column[k : k + 1]
-                for later in range(q + 1, width):
-                    part = panel[later][k : k + 1] * scale
-                    panel[later] = jnp.where(is_row, part, panel[later] - column * part)
-                line = jnp.where(is_lane[0:1], 1.0, m[k : k + 1]) * scale
-                packs[at] = jnp.where(is_row, line, jnp.where(is_lane, 0.0, m) - column * line)
-    return packs
-
-
 NODES = COL - 1
 
 
@@ -410,11 +382,7 @@
         held = {k: nodes[k] for k in range(0, NODES, stride)}
         links_now = {k: (links[k], turned[k]) for k in range(0, NODES - stride, stride)}
         gone = list(range(stride, NODES, 2 * stride))
-        if len(gone) == 4:
-            [pack] = inverse([jnp.concatenate([held[k] for k in gone], axis=1)], 16)
-            solved = [pack[:, at * K : (at + 1) * K] for at in range(4)]
-        else:
-            solved = inverses([held[k] for k in gone], 16)
+        solved = inverses([held[k] for k in gone], 8)
         eliminate(stride, held, gone, links_now, solved)
 
     for stride in (2, 4, 8):

time: 29.7 us -> 28.5 us (0.960)
  local copies, waits for them, and re-layouts: 0.94 us -> 0 us
    unnamed x2 -> x0, local copies, waits for them, and re-layouts: 0.94 us -> none
    pallas_call x1, Pallas kernels: 20.3 us -> 19.4 us  [made_blocks(): pl.pallas_call(blocks_kernel, out_shape=pltpu.VMEM((COL, K, 4 * K), F32),...]
    pallas_call x1, Pallas kernels: 7.66 us -> 8.29 us  [local(): pl.pallas_call(chain_kernel, out_shape=(jax.ShapeDtypeStruct((1, 1, 3, K,...]
where the time goes in v4:
time: 28.5 us; the launch traced here: 28.3 us
  Pallas kernels  27.7 us (97%)
  between operations  0.64 us (2%)
    pallas_call x1, Pallas kernels, made_blocks(): pl.pallas_call(blocks_kernel, out_shape=pltpu.VMEM((COL, K, 4 * K), F32),...  19.4 us
    pallas_call x1, Pallas kernels, local(): pl.pallas_call(chain_kernel, out_shape=(jax.ShapeDtypeStruct((1, 1, 3, K,...  8.29 us

profile of v4, /device:TPU:6, one launch (start us, length us, event | category | flops | bytes accessed | tf_op | source)
XLA Modules:
  0.0 28.3 jit_solution(17744677693557924559)
XLA Ops:
  0.6 19.4 %shard_map.85.got_ref = f32[16,32,128]{2,1,0:T(8,128)S(1)} custom-call(f32[1,1,32,16384]{3,2,1,0:T(8,128)} %defl_hbm.1, f32[1,1,16384]{2,1,0:T(1,128)} %diag_ref.1, bf16[1,1,128,2,128,128]{5,4,3,2,1,0:T(8,128)(2,1)} %vals_hbm.1, s32[1,1,2,128]{3,2,1,0:T(2,128)} %bitcast.1, bf16[1,1,32,128,128]{4,3,2,1,0:T(8,128)(2,1)} %west_hbm.1, ...), custom_call_target="tpu_custom_call" | custom-call | tf_op jit(solution)/shard_map/pallas_call | solution.py:296
  20.0 8.3 %shard_map.86 = (f32[1,1,3,32,32]{4,3,2,1,0:T(8,128)}, f32[1,1,32,32]{3,2,1,0:T(8,128)}, f32[1,1,32,32]{3,2,1,0:T(8,128)}) custom-call(f32[16,32,128]{2,1,0:T(8,128)S(1)} %shard_map.85.got_ref), custom_call_target="tpu_custom_call" | custom-call | tf_op jit(solution)/shard_map/pallas_call | solution.py:399

commit v5 on v4

--- a/solution.py
+++ b/solution.py
@@ -334,63 +334,60 @@
 NODES = COL - 1
 
 
-def chain_kernel(got_ref, coarse_ref, pivot_ref, mult_ref, nodes, links, turned):
+def chain_kernel(got_ref, coarse_ref, pivot_ref, mult_ref):
     col = lax.axis_index("gy")
-    own = got_ref[COL - 1]
-    self_own = own[:, 0:K]
-    west_own = (own + got_ref[0])[:, K : 2 * K]
-    west_own = jnp.where(col > 0, west_own, 0.0)
-    coarse_ref[0, 0, 0] = self_own
-    coarse_ref[0, 0, 1] = west_own
-    coarse_ref[0, 0, 2] = own[:, 2 * K : 3 * K]
     eye = (
         lax.broadcasted_iota(jnp.int32, (K, K), 0) == lax.broadcasted_iota(jnp.int32, (K, K), 1)
     ).astype(F32)
-    nodes[0] = jnp.where(col > 0, got_ref[0][:, 0:K], eye)
-
-    def eliminate(stride, held, gone, links_now, solved):
-        for k, inv in zip(gone, solved, strict=True):
-            near = links_now[k - stride][0]
-            if k + stride < NODES:
-                far, far_t = links_now[k]
+
+    def eliminate(stride, held, links, solved):
+        fresh = {}
+        for k, inv in solved.items():
+            near = links[k - stride][0]
+            if k + stride in held:
+                far, far_t = links[k]
                 outer = exact(jnp.concatenate([near, far_t], axis=0), inv)
                 to_near = exact_nt(outer, near)
                 to_far = exact(outer, far)
                 held[k - stride] = held[k - stride] - to_near[0:K]
                 held[k + stride] = held[k + stride] - to_far[K : 2 * K]
-                links[k - stride] = -to_far[0:K]
-                turned[k - stride] = -to_near[K : 2 * K]
+                fresh[k - stride] = (-to_far[0:K], -to_near[K : 2 * K])
             else:
                 held[k - stride] = held[k - stride] - exact_nt(exact(near, inv), near)
-        for k in range(0, NODES, 2 * stride):
-            nodes[k] = held[k]
-
-    @pl.when(col > 1)
-    def _():
-        held = {k: jnp.where(k < col, got_ref[k][:, 0:K], eye) for k in range(0, NODES, 2)}
-        links_now = {}
-        for k in range(NODES - 1):
+        return {k: held[k] for k in held if k not in solved}, fresh
+
+    def solve(count):
+        own = got_ref[COL - 1]
+        self_own = own[:, 0:K]
+        west_own = (own + got_ref[0])[:, K : 2 * K]
+        west_own = jnp.where(col > 0, west_own, 0.0)
+        coarse_ref[0, 0, 0] = self_own
+        coarse_ref[0, 0, 1] = west_own
+        coarse_ref[0, 0, 2] = own[:, 2 * K : 3 * K]
+        held = {k: jnp.where(k < col, got_ref[k][:, 0:K], eye) for k in range(0, count, 2)}
+        links = {}
+        for k in range(count - 1):
             both = got_ref[k] + got_ref[k + 1]
             if k % 2:
-                links_now[k] = (both[:, K : 2 * K], both[:, 3 * K : 4 * K])
+                links[k] = (both[:, K : 2 * K], both[:, 3 * K : 4 * K])
             else:
-                links_now[k] = (both[:, 2 * K : 3 * K],)
-        gone = list(range(1, NODES, 2))
-        eliminate(1, held, gone, links_now, [got_ref[k][:, 0:K] for k in gone])
-
-    def level(stride):
-        held = {k: nodes[k] for k in range(0, NODES, stride)}
-        links_now = {k: (links[k], turned[k]) for k in range(0, NODES - stride, stride)}
-        gone = list(range(stride, NODES, 2 * stride))
-        solved = inverses([held[k] for k in gone], 8)
-        eliminate(stride, held, gone, links_now, solved)
-
-    for stride in (2, 4, 8):
-        pl.when(col > stride)(functools.partial(level, stride))
-    [last] = inverses([nodes[0]], 16)
-    mult = exact(west_own, last)
-    pivot_ref[0, 0] = self_own - exact_nt(mult, west_own)
-    mult_ref[0, 0] = mult
+                links[k] = (both[:, 2 * K : 3 * K],)
+        odd = {k: got_ref[k][:, 0:K] for k in range(1, count, 2)}
+        full, links = eliminate(1, held, links, odd)
+        stride = 2
+        while stride < count:
+            gone = list(range(stride, count, 2 * stride))
+            solved = inverses([full[k] for k in gone], 8)
+            full, links = eliminate(stride, full, links, dict(zip(gone, solved, strict=True)))
+            stride *= 2
+        [last] = inverses([full[0]], 16)
+        mult = exact(west_own, last)
+        pivot_ref[0, 0] = self_own - exact_nt(mult, west_own)
+        mult_ref[0, 0] = mult
+
+    pl.when(col <= 4)(functools.partial(solve, 4))
+    pl.when(jnp.logical_and(col > 4, col <= 8))(functools.partial(solve, 8))
+    pl.when(col > 8)(functools.partial(solve, NODES))
 
 
 def local(defl, diag, vals, cols, west, north):
@@ -405,7 +402,6 @@
         ),
         in_specs=[vmem],
         out_specs=(vmem, vmem, vmem),
-        scratch_shapes=[pltpu.VMEM((NODES, K, K), F32)] * 3,
         compiler_params=pltpu.CompilerParams(vmem_limit_bytes=16 * 2**20),
     )(got)
 

time: 28.5 us -> 27.5 us (0.965)
  Pallas kernels: 27.7 us -> 26.6 us
    pallas_call x1, Pallas kernels: 8.29 us -> 7.21 us  [local(): pl.pallas_call(chain_kernel, out_shape=(jax.ShapeDtypeStruct((1, 1, 3, K,...]
where the time goes in v5:
time: 27.5 us; the launch traced here: 27.2 us
  Pallas kernels  26.6 us (97%)
  between operations  0.64 us (2%)
    pallas_call x1, Pallas kernels, made_blocks(): pl.pallas_call(blocks_kernel, out_shape=pltpu.VMEM((COL, K, 4 * K), F32),...  19.4 us
    pallas_call x1, Pallas kernels, local(): pl.pallas_call(chain_kernel, out_shape=(jax.ShapeDtypeStruct((1, 1, 3, K,...  7.21 us

profile of v5, /device:TPU:6, one launch (start us, length us, event | category | flops | bytes accessed | tf_op | source)
XLA Modules:
  0.0 27.2 jit_solution(16111866318148077082)
XLA Ops:
  0.6 19.4 %shard_map.85.got_ref = f32[16,32,128]{2,1,0:T(8,128)S(1)} custom-call(f32[1,1,32,16384]{3,2,1,0:T(8,128)} %defl_hbm.1, f32[1,1,16384]{2,1,0:T(1,128)} %diag_ref.1, bf16[1,1,128,2,128,128]{5,4,3,2,1,0:T(8,128)(2,1)} %vals_hbm.1, s32[1,1,2,128]{3,2,1,0:T(2,128)} %bitcast.1, bf16[1,1,32,128,128]{4,3,2,1,0:T(8,128)(2,1)} %west_hbm.1, ...), custom_call_target="tpu_custom_call" | custom-call | tf_op jit(solution)/shard_map/pallas_call | solution.py:296
  20.0 7.2 %shard_map.86 = (f32[1,1,3,32,32]{4,3,2,1,0:T(8,128)}, f32[1,1,32,32]{3,2,1,0:T(8,128)}, f32[1,1,32,32]{3,2,1,0:T(8,128)}) custom-call(f32[16,32,128]{2,1,0:T(8,128)S(1)} %shard_map.85.got_ref), custom_call_target="tpu_custom_call" | custom-call | tf_op jit(solution)/shard_map/pallas_call | solution.py:396
